TPU v7x, 256 devices: a whole 4x4x8 slice. The times are simulated.
256 devices in a mesh: frames: 32 (over z_hi, y, core), heads: 8 (over z_lo, x).
Axes of the slice: x: 4, y: 4, z: 8 (z_hi: 4, z_lo: 2; z = z_hi * 2 + z_lo), core: 2. Of those that a mesh axis runs over, the one named last changes fastest.
Arguments:
- span_qkv: bfloat16 [3, 2304, 5120], P(None, ('frames', 'heads')), may hold values from -64 to 64
- history_kv: bfloat16 [2, 6144, 5120], P(None, 'frames', 'heads'), may hold values from -4 to 4
Outputs:
- attended: bfloat16 [2304, 5120], P(('frames', 'heads'))
All inputs are finite; a program needn't handle non-finite values.
Results may differ from a plain program's by a relative error of at most 0.017.
Values may be sent and summed in bfloat16 or wider, within the bound.
No kernel may reach another device: no remote copies, remote signals or barrier semaphores. Data moves between devices by JAX's collectives and lax.ppermute only.
A program may use at most 128 MiB of HBM per device.

v0:
```python
import math

import jax
import jax.numpy as jnp
from jax import lax
from jax.sharding import PartitionSpec as P

HEADS = 40
HEAD_DIM = 128
SPAN_FRAMES = 3


def head_scores(carry, queries, keys, values, allowed, scale):
    largest, total, summed = carry
    score = jnp.einsum("qd,kd->qk", queries, keys, preferred_element_type=jnp.float32) * scale
    if allowed is not None:
        score = jnp.where(allowed, score, -1e30)
    newest = jnp.maximum(largest, jnp.max(score, axis=1))
    factor = jnp.exp(largest - newest)
    weight = jnp.exp(score - newest[:, None])
    total = total * factor + jnp.sum(weight, axis=1)
    summed = summed * factor[:, None] + jnp.dot(
        weight.astype(jnp.bfloat16), values, preferred_element_type=jnp.float32
    )
    return (newest, total, summed)


def on_device(span_qkv, history_kv):
    frame_count = lax.axis_size("frames")
    heads_here = HEADS // lax.axis_size("heads")
    scale = 1.0 / math.sqrt(HEAD_DIM)
    local = lax.all_to_all(span_qkv, "heads", split_axis=2, concat_axis=1, tiled=True)
    rows = local.shape[1]
    tokens_all = rows * frame_count
    frame_len = tokens_all // SPAN_FRAMES
    first = lax.axis_index("frames") * rows
    query_frame = (first + jnp.arange(rows, dtype=jnp.int32)) // frame_len
    queries = local[0]

    def fold_heads(carry, piece, allowed):
        updated = []
        for head in range(heads_here):
            low = head * HEAD_DIM
            high = low + HEAD_DIM
            updated.append(
                head_scores(
                    carry[head],
                    queries[:, low:high],
                    piece[0][:, low:high],
                    piece[1][:, low:high],
                    allowed,
                    scale,
                )
            )
        return tuple(updated)

    initial = tuple(
        (
            (
                jnp.full((rows,), -1e30, jnp.float32),
                jnp.zeros((rows,), jnp.float32),
                jnp.zeros((rows, HEAD_DIM), jnp.float32),
            )
            for head in range(heads_here)
        )
    )
    carry = fold_heads(initial, lax.all_gather(history_kv, "frames", axis=1, tiled=True), None)
    piece = lax.all_gather(local[1:3], "frames", axis=1, tiled=True)
    count = piece.shape[1]
    key_frame = jnp.arange(count, dtype=jnp.int32) // frame_len
    allowed = query_frame[:, None] >= key_frame[None, :]
    carry = fold_heads(carry, piece, allowed)
    result = jnp.concatenate(
        [carry[head][2] / carry[head][1][:, None] for head in range(heads_here)], axis=1
    ).astype(jnp.bfloat16)
    return lax.all_to_all(result, "heads", split_axis=0, concat_axis=1, tiled=True)


def solution(mesh):
    in_specs = (P(None, ("frames", "heads"), None), P(None, "frames", "heads"))
    out_specs = P(("frames", "heads"), None)
    return jax.shard_map(
        on_device, mesh=mesh, in_specs=in_specs, out_specs=out_specs, check_vma=False
    )
```

profile of v0, /device:TPU:8, one launch (start us, length us, event | category | flops | bytes accessed | tf_op | source)
XLA Modules:
  0.0 299.0 jit_solution(2809273356933714019)
XLA Ops:
  6.5 6.5 %copy.12 = bf16[3,9,5120]{1,0,2:T(4,128)(2,1)} copy(bf16[3,9,5120]{2,0,1:T(4,128)(2,1)} %param.2) | data formatting | bytes 552960 | tf_op args[0]
  13.0 7.6 %reshape.192 = bf16[8,2,8640]{2,1,0:T(2,128)(2,1)S(1)} reshape(bf16[5120,3,9]{2,1,0:T(4,128)(2,1)} %bitcast.18) | data formatting | bytes 552960
  20.6 13.1 %all_to_all.31 = bf16[8,2,8640]{2,1,0:T(2,128)(2,1)S(1)} all-to-all(bf16[8,2,8640]{2,1,0:T(2,128)(2,1)S(1)} %reshape.192), channel_id=1, replica_groups=mesh['frames'=32,'heads'=8] {'heads'}, dimensions={0} | all-to-all | bytes 552960 | tf_op jit(solution)/shard_map/all_to_all | solution.py:32
  33.7 6.2 %reshape.193 = bf16[5120,3,9]{2,1,0:T(4,128)(2,1)} reshape(bf16[8,2,8640]{2,1,0:T(2,128)(2,1)S(1)} %all_to_all.31) | data formatting | bytes 552960
  40.0 6.7 %copy.13 = bf16[3,9,8,640]{3,0,1,2:T(4,128)(2,1)S(1)} copy(bf16[3,9,8,640]{1,0,3,2:T(4,128)(2,1)} %bitcast.17) | data formatting | bytes 552960 | tf_op jit(solution)/shard_map/all_to_all | solution.py:32
  49.0 66.2 %all-gather.5.cloned.1.call-done = bf16[2,2304,640]{2,0,1:T(2,128)(2,1)} async-done(((bf16[2,72,640]{2,0,1:T(2,128)(2,1)}), bf16[2,2304,640]{2,0,1:T(2,128)(2,1)}) %all-gather.5.cloned.1.call-update) | async-done | bytes 5898256 | tf_op jit(solution)/shard_map/all_gather | solution.py:68
  115.2 12.2 %fusion.128 = (bf16[1,2304,640]{2,0,1:T(2,128)(2,1)S(1)}, bf16[1,2304,640]{2,0,1:T(2,128)(2,1)S(1)}) fusion(bf16[2,2304,640]{2,0,1:T(2,128)(2,1)} %all-gather.5.cloned.1.call-done), kind=kLoop, calls=%fused_computation.158 | loop fusion | bytes 11796480 | tf_op jit(solution)/shard_map/slice | solution.py:50
  127.4 3.5 %copy_bitcast_fusion = (bf16[2304,640]{1,0:T(8,128)(2,1)}, bf16[2304,640]{1,0:T(8,128)(2,1)}) fusion(bf16[1,2304,640]{2,0,1:T(2,128)(2,1)S(1)} %get-tuple-element.17, bf16[1,2304,640]{2,0,1:T(2,128)(2,1)S(1)} %get-tuple-element.18), kind=kLoop, calls=%fused_computation.17 | loop fusion | bytes 11796480 | tf_op jit(solution)/shard_map/squeeze | solution.py:50
  130.9 3.1 %fusion.138 = (f32[72]{0:T(128)}, f32[72,2304]{1,0:T(8,128)}) fusion(bf16[2304,640]{1,0:T(8,128)(2,1)} %get-tuple-element.55, bf16[72,640]{1,0:T(8,128)(2,1)S(1)} %squeeze.10, s32[2304]{0:T(1024)S(1)} %add_select_fusion, s32[72]{0:T(128)S(1)} %and_select_fusion), kind=kOutput, calls=%fused_computation.168 | convolution fusion | flops 43130808 | bytes 1284896 | tf_op jit(solution)/shard_map/qd,kd->qk/dot_general | solution.py:15
  134.0 3.1 %fusion.136 = (f32[72]{0:T(128)}, f32[72,2304]{1,0:T(8,128)}) fusion(bf16[2304,640]{1,0:T(8,128)(2,1)} %get-tuple-element.55, bf16[72,640]{1,0:T(8,128)(2,1)S(1)} %squeeze.10, s32[2304]{0:T(1024)S(1)} %add_select_fusion, s32[72]{0:T(128)S(1)} %and_select_fusion), kind=kOutput, calls=%fused_computation.166 | convolution fusion | flops 43130808 | bytes 1284896 | tf_op jit(solution)/shard_map/qd,kd->qk/dot_general | solution.py:15
  137.1 3.1 %fusion.134 = (f32[72]{0:T(128)}, f32[72,2304]{1,0:T(8,128)}) fusion(bf16[2304,640]{1,0:T(8,128)(2,1)} %get-tuple-element.55, bf16[72,640]{1,0:T(8,128)(2,1)S(1)} %squeeze.10, s32[2304]{0:T(1024)S(1)} %add_select_fusion, s32[72]{0:T(128)S(1)} %and_select_fusion), kind=kOutput, calls=%fused_computation.164 | convolution fusion | flops 43130808 | bytes 1284896 | tf_op jit(solution)/shard_map/qd,kd->qk/dot_general | solution.py:15
  140.2 3.1 %fusion.132 = (f32[72]{0:T(128)}, f32[72,2304]{1,0:T(8,128)}) fusion(bf16[2304,640]{1,0:T(8,128)(2,1)} %get-tuple-element.55, bf16[72,640]{1,0:T(8,128)(2,1)S(1)} %squeeze.10, s32[2304]{0:T(1024)S(1)} %add_select_fusion, s32[72]{0:T(128)S(1)} %and_select_fusion), kind=kOutput, calls=%fused_computation.162 | convolution fusion | flops 43130808 | bytes 1284896 | tf_op jit(solution)/shard_map/qd,kd->qk/dot_general | solution.py:15
  143.2 3.0 %fusion.130 = (f32[72]{0:T(128)}, f32[72,2304]{1,0:T(8,128)}) fusion(bf16[2304,640]{1,0:T(8,128)(2,1)} %get-tuple-element.55, bf16[72,640]{1,0:T(8,128)(2,1)S(1)} %squeeze.10, s32[2304]{0:T(1024)S(1)} %add_select_fusion, s32[72]{0:T(128)S(1)} %and_select_fusion), kind=kOutput, calls=%fused_computation.160 | convolution fusion | flops 43130808 | bytes 1284896 | tf_op jit(solution)/shard_map/qd,kd->qk/dot_general | solution.py:15
  146.3 70.2 %all-gather.3.cloned.1.call-done = bf16[2,6144,640]{2,1,0:T(8,128)(2,1)} async-done(((bf16[2,192,640]{2,1,0:T(8,128)(2,1)}), bf16[2,6144,640]{2,1,0:T(8,128)(2,1)}) %all-gather.3.cloned.1.call-update) | async-done | bytes 15728656 | tf_op jit(solution)/shard_map/all_gather | solution.py:67
  216.5 6.5 %slice_bitcast_fusion.1 = (bf16[6144,640]{1,0:T(8,128)(2,1)S(1)}, bf16[6144,640]{1,0:T(8,128)(2,1)S(1)}) fusion(bf16[2,6144,640]{2,1,0:T(8,128)(2,1)} %all-gather.3.cloned.1.call-done), kind=kLoop, calls=%fused_computation.1 | loop fusion | bytes 31457280 | tf_op jit(solution)/shard_map/squeeze | solution.py:49
  224.2 2.6 fusion.135
  226.8 2.5 fusion.133
  233.8 2.0 fusion.69
  243.9 2.0 fusion.68
  250.7 2.0 fusion.50
  252.7 2.0 fusion.67
  257.9 2.0 fusion.38
  263.2 2.0 fusion.44
  266.8 24.7 %all_to_all.32 = bf16[8,9,640]{2,1,0:T(8,128)(2,1)S(1)} all-to-all(bf16[8,9,640]{2,1,0:T(8,128)(2,1)S(1)} %constant_dynamic-update-slice_fusion), channel_id=1, replica_groups=mesh['frames'=32,'heads'=8] {'heads'}, dimensions={0} | all-to-all | bytes 184320 | tf_op jit(solution)/shard_map/all_to_all | solution.py:76
  (81 shorter events, 29.2 us)
Async XLA Ops:
  6.5 108.6 %all-gather.5.cloned.1.call-start = ((), (), s32[]{:S(2)}) async-start(), calls=%async_computation.3 | async-start | bytes 6082560 | tf_op jit(solution)/shard_map/all_gather | solution.py:68
  47.6 168.8 %all-gather.3.cloned.1.call-start = ((), (), s32[]{:S(2)}) async-start(), calls=%async_computation.2 | async-start | bytes 16220160 | tf_op jit(solution)/shard_map/all_gather | solution.py:67
  49.0 180.3 %copy-start.8 = (bf16[72,640]{1,0:T(8,128)(2,1)}, bf16[72,640]{1,0:T(8,128)(2,1)S(1)}, u32[]{:S(2)}) copy-start(bf16[72,640]{1,0:T(8,128)(2,1)S(1)} %squeeze.10) | copy-start | bytes 276484
  223.0 10.2 %copy-start = (bf16[6144,640]{1,0:T(8,128)(2,1)}, bf16[6144,640]{1,0:T(8,128)(2,1)S(1)}, u32[]{:S(2)}) copy-start(bf16[6144,640]{1,0:T(8,128)(2,1)S(1)} %get-tuple-element.16) | copy-start | bytes 23592964
  230.5 2.0 copy-start.15
  230.5 2.0 copy-start.7
  237.1 4.9 %copy-start.2 = (f32[72,6144]{1,0:T(8,128)S(1)}, f32[72,6144]{1,0:T(8,128)}, u32[]{:S(2)}) copy-start(f32[72,6144]{1,0:T(8,128)} %get-tuple-element.47) | copy-start | bytes 5308420
  241.2 2.7 copy-start.6
  242.0 5.3 %copy-start.14 = (f32[72]{0:T(128)S(1)}, f32[72]{0:T(128)}, u32[]{:S(2)}) copy-start(f32[72]{0:T(128)} %get-tuple-element.44) | copy-start | bytes 868
  247.3 3.4 %copy-start.1 = (f32[72,6144]{1,0:T(8,128)S(1)}, f32[72,6144]{1,0:T(8,128)}, u32[]{:S(2)}) copy-start(f32[72,6144]{1,0:T(8,128)} %get-tuple-element.43) | copy-start | bytes 5308420
  250.7 2.1 copy-start.5
  250.7 5.4 %copy-start.13 = (f32[72]{0:T(128)S(1)}, f32[72]{0:T(128)}, u32[]{:S(2)}) copy-start(f32[72]{0:T(128)} %get-tuple-element.36) | copy-start | bytes 868
  257.9 2.0 copy-start.4
  257.9 3.4 %copy-start.12 = (f32[72]{0:T(128)S(1)}, f32[72]{0:T(128)}, u32[]{:S(2)}) copy-start(f32[72]{0:T(128)} %get-tuple-element.40) | copy-start | bytes 868
  263.2 2.1 copy-start.3
  263.2 3.5 %copy-start.11 = (bf16[8,9,128]{2,1,0:T(8,128)(2,1)S(1)}, bf16[8,9,128]{2,1,0:T(8,128)(2,1)}, u32[]{:S(2)}) copy-start(bf16[8,9,128]{2,1,0:T(8,128)(2,1)} %concatenate.17) | copy-start | bytes 55300
  263.2 3.5 %copy-start.10 = (bf16[8,9,128]{2,1,0:T(8,128)(2,1)S(1)}, bf16[8,9,128]{2,1,0:T(8,128)(2,1)}, u32[]{:S(2)}) copy-start(bf16[8,9,128]{2,1,0:T(8,128)(2,1)} %concatenate.18) | copy-start | bytes 55300
  263.2 3.5 %copy-start.9 = (bf16[8,9,128]{2,1,0:T(8,128)(2,1)S(1)}, bf16[8,9,128]{2,1,0:T(8,128)(2,1)}, u32[]{:S(2)}) copy-start(bf16[8,9,128]{2,1,0:T(8,128)(2,1)} %concatenate.19) | copy-start | bytes 55300
Sparse Core Ops, SparseCore 0:
  47.7 67.3 all-gather.4
  117.8 98.6 all-gather.2
where the time goes:
time: 301 us; the launch traced here: 299 us
  waiting for transfers between devices  137 us (46%)
  local copies, waits for them, and re-layouts  55.7 us (19%)
  matrix products  42 us (14%)
  blocking collectives  37.9 us (13%)
  between operations  13.8 us (5%)
  other arithmetic  12.6 us (4%)
    all_gather x1, waiting for transfers between devices, on_device(): lax.all_gather(history_kv, 'frames', axis=1, tiled=True)  70.2 us
    all_gather x1, waiting for transfers between devices, on_device(): piece = lax.all_gather(local[1:3], 'frames', axis=1, tiled=True)  66.2 us
    dot_general x10, matrix products, head_scores(): jnp.einsum('qd,kd->qk', queries, keys, preferred_element_type=jnp.float32)  24.7 us
    all_to_all x1, blocking collectives, on_device(): lax.all_to_all(result, 'heads', split_axis=0, concat_axis=1, tiled=True)  24.7 us
    unnamed x41, local copies, waits for them, and re-layouts  21.1 us
    dot_general x10, matrix products, head_scores(): jnp.dot(weight.astype(jnp.bfloat16), values, preferred_element_type=jnp.f...  17.2 us
    all_to_all x1, blocking collectives, on_device(): lax.all_to_all(span_qkv, 'heads', split_axis=2, concat_axis=1, tiled=True)  13.1 us
    slice x1, local copies, waits for them, and re-layouts, fold_heads(): piece[1][:, low:high]  12.2 us
  transfers between devices with their start and end apart: 2, of which 2 were waited for; matrix products, arithmetic and copies ran while one was open for 11% of the time, Pallas kernels for 0%

commit v1 on v0

v1 whole, which is shorter than its diff:
```python
import math

import jax
import jax.numpy as jnp
from jax import lax
from jax.experimental import pallas as pl
from jax.experimental.pallas import tpu as pltpu
from jax.sharding import Mesh, PartitionSpec as P

HEADS = 40
HEAD_DIM = 128
TOKENS = 2304
HIST = 6144
FRAME_LEN = 768

FRAMES = ("zh", "y", "c")
GROUPS = ("zl", "x")
NZ, NY, NC, NG = 4, 4, 2, 8
HERE = HEADS // NG
WIDE = HERE * HEAD_DIM
HOME = TOKENS // (NZ * NY * NC * NG)
OWN = HOME * NG
PAD = 80
HKEYS = HIST // (NZ * NY * NC)
CHUNK = 48
ROWS = HERE * HOME
SENT = 32
SCALE = math.log2(math.e) / math.sqrt(HEAD_DIM)
F32, BF16 = jnp.float32, jnp.bfloat16
VMEM_LIMIT = 48 * 2**20


def params():
    return pltpu.CompilerParams(vmem_limit_bytes=VMEM_LIMIT)


def in_vmem(count):
    return [pl.BlockSpec(memory_space=pltpu.VMEM)] * count


def pack_kernel(x_ref, o_ref, scratch):
    scratch[...] = jnp.zeros_like(scratch)
    for g in range(NG):
        for i in range(3):
            piece = x_ref[i, :, g * WIDE : (g + 1) * WIDE]
            scratch[g, i * HOME : (i + 1) * HOME, :] = piece.astype(F32)
        o_ref[g] = scratch[g].astype(BF16)


def pack(x):
    return pl.pallas_call(
        pack_kernel,
        out_shape=jax.ShapeDtypeStruct((NG, SENT, WIDE), BF16),
        in_specs=in_vmem(1),
        out_specs=pl.BlockSpec(memory_space=pltpu.VMEM),
        scratch_shapes=[pltpu.VMEM((NG, SENT, WIDE), F32)],
        compiler_params=params(),
    )(x)


def unpack_kernel(x_ref, q_ref, kv_ref, scratch):
    scratch[...] = jnp.zeros_like(scratch)
    for g in range(NG):
        piece = x_ref[g].astype(F32)
        for i in range(3):
            scratch[i, g * HOME : (g + 1) * HOME, :] = piece[i * HOME : (i + 1) * HOME]
    q_ref[...] = scratch[0].astype(BF16)
    kv_ref[0] = scratch[1].astype(BF16)
    kv_ref[1] = scratch[2].astype(BF16)


def unpack(x):
    return pl.pallas_call(
        unpack_kernel,
        out_shape=(
            jax.ShapeDtypeStruct((PAD, WIDE), BF16),
            jax.ShapeDtypeStruct((2, PAD, WIDE), BF16),
        ),
        in_specs=in_vmem(1),
        out_specs=tuple(in_vmem(2)),
        scratch_shapes=[pltpu.VMEM((3, PAD, WIDE), F32)],
        compiler_params=params(),
    )(x)


QROWS = NZ * PAD
NHIST = NY * NC * HKEYS
NSPAN = NY * NC * PAD


def attend_kernel(place, *refs):
    qs = refs[:NZ]
    hist = refs[NZ : NZ + NY * NC]
    span = refs[NZ + NY * NC : NZ + 2 * NY * NC]
    o_ref = refs[NZ + 2 * NY * NC]
    q_all, k_all, v_all, part, chunks, stats = refs[NZ + 2 * NY * NC + 1 :]
    head = pl.program_id(0)
    zh, y, c = place[0], place[1], place[2]

    @pl.when(head == 0)
    def _():
        stats[...] = jnp.zeros_like(stats)

    for dz in range(NZ):
        q_all[dz * PAD : (dz + 1) * PAD, :] = qs[dz][...]
    for n in range(NY * NC):
        k_all[n * HKEYS : (n + 1) * HKEYS, :] = hist[n][0]
        v_all[n * HKEYS : (n + 1) * HKEYS, :] = hist[n][1]
        low = NHIST + n * PAD
        k_all[low : low + PAD, :] = span[n][0]
        v_all[low : low + PAD, :] = span[n][1]
    score = lax.dot_general(
        q_all[...], k_all[...], (((1,), (1,)), ((), ())), preferred_element_type=F32
    )

    row = lax.broadcasted_iota(jnp.int32, (QROWS, 1), 0)
    q_zh = lax.rem(zh + NZ - row // PAD, NZ)
    q_token = (q_zh * NY * NC + y * NC + c) * OWN + lax.rem(row, PAD)
    col = lax.broadcasted_iota(jnp.int32, (1, NSPAN), 1)
    block = col // PAD
    inside = lax.rem(col, PAD)
    k_y = lax.rem(y + NY - block // NC, NY)
    k_c = jnp.where(lax.rem(block, NC) == 0, c, 1 - c)
    k_token = (zh * NY * NC + k_y * NC + k_c) * OWN + inside
    k_frame = jnp.where(inside < OWN, k_token // FRAME_LEN, TOKENS)
    allowed = q_token // FRAME_LEN >= k_frame

    s_hist = score[:, :NHIST]
    s_span = jnp.where(allowed, score[:, NHIST:], -1e30)
    top = jnp.maximum(
        jnp.max(s_hist, axis=1, keepdims=True), jnp.max(s_span, axis=1, keepdims=True)
    )
    w_hist = jnp.exp2((s_hist - top) * SCALE)
    w_span = jnp.exp2((s_span - top) * SCALE)
    total = jnp.sum(w_hist, axis=1, keepdims=True) + jnp.sum(w_span, axis=1, keepdims=True)
    summed = jnp.dot(
        w_hist.astype(BF16), v_all[:NHIST, :], preferred_element_type=F32
    ) + jnp.dot(w_span.astype(BF16), v_all[NHIST:, :], preferred_element_type=F32)
    part[...] = summed / total

    for dz in range(NZ):
        home_z = lax.rem(zh + NZ - dz, NZ)
        for g in range(NG):
            low = dz * PAD + g * HOME
            chunks[home_z * NG + g, pl.ds(head * HOME, HOME), :] = part[low : low + HOME, :]

    lse = top * SCALE + jnp.log2(total)
    high = lse.astype(BF16).astype(F32)
    middle = (lse - high).astype(BF16).astype(F32)
    low_term = lse - high - middle
    token = lax.rem(row, PAD)
    lane = lax.broadcasted_iota(jnp.int32, (QROWS, HEAD_DIM), 1)
    here = (lane == head * HOME + lax.rem(token, HOME)) & (token < OWN)
    to_chunk = lax.broadcasted_iota(jnp.int32, (NZ * NG, QROWS), 0)
    from_row = lax.broadcasted_iota(jnp.int32, (NZ * NG, QROWS), 1)
    from_z = lax.rem(zh + NZ - from_row // PAD, NZ)
    pick = (to_chunk == from_z * NG + lax.rem(from_row, PAD) // HOME).astype(F32).astype(BF16)
    for n, term in enumerate((high, middle, low_term)):
        spread = jnp.where(here, term, 0.0).astype(BF16)
        stats[n] += jnp.dot(pick, spread, preferred_element_type=F32)

    @pl.when(head == HERE - 1)
    def _():
        for n in range(3):
            for chunk in range(NZ * NG):
                chunks[chunk, ROWS + n : ROWS + n + 1, :] = stats[n, chunk : chunk + 1, :]
        o_ref[...] = chunks[...].astype(BF16)


def attend(place, qs, hist, span):
    q_spec = pl.BlockSpec((PAD, HEAD_DIM), lambda h, p: (0, h))
    hist_spec = pl.BlockSpec((2, HKEYS, HEAD_DIM), lambda h, p: (0, 0, h))
    span_spec = pl.BlockSpec((2, PAD, HEAD_DIM), lambda h, p: (0, 0, h))
    keys = NHIST + NSPAN
    return pl.pallas_call(
        attend_kernel,
        out_shape=jax.ShapeDtypeStruct((NZ * NG, CHUNK, HEAD_DIM), BF16),
        grid_spec=pltpu.PrefetchScalarGridSpec(
            num_scalar_prefetch=1,
            grid=(HERE,),
            in_specs=[q_spec] * NZ + [hist_spec] * (NY * NC) + [span_spec] * (NY * NC),
            out_specs=pl.BlockSpec((NZ * NG, CHUNK, HEAD_DIM), lambda h, p: (0, 0, 0)),
            scratch_shapes=[
                pltpu.VMEM((QROWS, HEAD_DIM), BF16),
                pltpu.VMEM((keys, HEAD_DIM), BF16),
                pltpu.VMEM((keys, HEAD_DIM), BF16),
                pltpu.VMEM((QROWS, HEAD_DIM), F32),
                pltpu.VMEM((NZ * NG, CHUNK, HEAD_DIM), F32),
                pltpu.VMEM((3, NZ * NG, HEAD_DIM), F32),
            ],
        ),
        compiler_params=params(),
        cost_estimate=pl.CostEstimate(
            flops=4 * QROWS * keys * WIDE,
            bytes_accessed=4 * keys * WIDE,
            transcendentals=QROWS * keys * HERE,
        ),
    )(place, *qs, *hist, *span)


def merge_kernel(x_ref, o_ref, rows):
    eye = lax.broadcasted_iota(jnp.int32, (CHUNK, HEAD_DIM), 0) == lax.broadcasted_iota(
        jnp.int32, (CHUNK, HEAD_DIM), 1
    )
    for g in range(NG):
        parts = [x_ref[z * NG + g].astype(F32) for z in range(NZ)]
        lses = [
            (p[ROWS : ROWS + 1] + p[ROWS + 1 : ROWS + 2]) + p[ROWS + 2 : ROWS + 3] for p in parts
        ]
        top = jnp.maximum(jnp.maximum(lses[0], lses[1]), jnp.maximum(lses[2], lses[3]))
        weights = [jnp.exp2(v - top) for v in lses]
        total = (weights[0] + weights[1]) + (weights[2] + weights[3])
        out = jnp.zeros((CHUNK, HEAD_DIM), F32)
        for p, w in zip(parts, weights):
            share = jnp.sum(jnp.where(eye, w / total, 0.0), axis=1, keepdims=True)
            out = out + share * p
        rows[g] = out
        for e in range(HERE):
            low = (g * HERE + e) * HEAD_DIM
            o_ref[:, low : low + HEAD_DIM] = rows[g, e * HOME : (e + 1) * HOME, :].astype(BF16)


def merge(x):
    return pl.pallas_call(
        merge_kernel,
        out_shape=jax.ShapeDtypeStruct((HOME, HEADS * HEAD_DIM), BF16),
        in_specs=in_vmem(1),
        out_specs=pl.BlockSpec(memory_space=pltpu.VMEM),
        scratch_shapes=[pltpu.VMEM((NG, CHUNK, HEAD_DIM), F32)],
        compiler_params=params(),
    )(x)


def from_back(x, axis, size, back):
    return lax.ppermute(x, axis, [(i, (i + back) % size) for i in range(size)])


def on_device(span_qkv, history_kv):
    place = jnp.stack([lax.axis_index(a) for a in FRAMES]).astype(jnp.int32)
    hist_y = [history_kv] + [from_back(history_kv, "y", NY, d) for d in (1, 2, 3)]
    hist = []
    for block in hist_y:
        hist += [block, from_back(block, "c", NC, 1)]
    local = lax.all_to_all(pack(span_qkv), GROUPS, split_axis=0, concat_axis=0, tiled=True)
    q, kv = unpack(local)
    qs = [q] + [from_back(q, "zh", NZ, d) for d in (1, 2, 3)]
    span_y = [kv] + [from_back(kv, "y", NY, d) for d in (1, 2, 3)]
    span = []
    for block in span_y:
        span += [block, from_back(block, "c", NC, 1)]
    partial = attend(place, qs, hist, span)
    home = lax.all_to_all(partial, ("zh",) + GROUPS, split_axis=0, concat_axis=0, tiled=True)
    return merge(home)


def solution(mesh):
    cut = Mesh(mesh.devices.reshape(NZ, NY, NC, 2, 4), FRAMES + GROUPS)
    in_specs = (P(None, FRAMES + GROUPS, None), P(None, FRAMES, GROUPS))
    out_specs = P(FRAMES + GROUPS, None)
    return jax.shard_map(
        on_device, mesh=cut, in_specs=in_specs, out_specs=out_specs, check_vma=False
    )
```

time: 301 us -> 99.5 us (0.33)
  waiting for transfers between devices: 137 us -> 23.6 us
  local copies, waits for them, and re-layouts: 55.7 us -> 8.92 us
  matrix products: 42 us -> 0 us
  starting transfers between devices: 0.04 us -> 27.2 us
  Pallas kernels: 0 us -> 14.5 us
  between operations: 13.8 us -> 0.06 us
  blocking collectives: 37.9 us -> 24.7 us
  other arithmetic: 12.6 us -> 0.08 us
    all_gather x2 -> x0, waiting for transfers between devices: 136 us -> none  [the longest x1 70.2 us: on_device(): lax.all_gather(history_kv, 'frames', axis=1, tiled=True)]
    dot_general x20 -> x0, matrix products: 42 us -> none  [the longest x10 24.7 us: head_scores(): jnp.einsum('qd,kd->qk', queries, keys, preferred_element_type=jnp.float32)]
    ppermute x0 -> x17, starting transfers between devices: none -> 21.4 us  [from_back(): return lax.ppermute(x, axis, [(i, (i + back) % size) for i in range(size)])]
    ppermute x0 -> x17, waiting for transfers between devices: none -> 20.2 us  [from_back(): return lax.ppermute(x, axis, [(i, (i + back) % size) for i in range(size)])]
    pallas_call x0 -> x4, Pallas kernels: none -> 14.5 us  [the longest x1 12.5 us: attend(): pl.pallas_call(attend_kernel, out_shape=jax.ShapeDtypeStruct((NZ * NG, CH...]
    slice x3 -> x0, local copies, waits for them, and re-layouts: 13.6 us -> none  [the longest x1 12.2 us: fold_heads(): piece[1][:, low:high]]
    all_to_all x2 -> x1, blocking collectives: 37.9 us -> 24.7 us  [on_device(): lax.all_to_all(partial, ('zh',) + GROUPS, split_axis=0, concat_axis=0, ti...]
    unnamed x41 -> x23, local copies, waits for them, and re-layouts: 21.1 us -> 8.92 us
  transfers between devices with their start and end apart: 2 -> 18, of which waited for: 2 -> 8; matrix products, arithmetic and copies ran while one was open for 11% -> 0% of each run, Pallas kernels for 0% -> 0%
where the time goes in v1:
time: 99.5 us; the launch traced here: 99 us
  starting transfers between devices  27.2 us (27%)
  blocking collectives  24.7 us (25%)
  waiting for transfers between devices  23.6 us (24%)
  Pallas kernels  14.5 us (15%)
  local copies, waits for them, and re-layouts  8.92 us (9%)
    all_to_all x1, blocking collectives, on_device(): lax.all_to_all(partial, ('zh',) + GROUPS, split_axis=0, concat_axis=0, ti...  24.7 us
    ppermute x17, starting transfers between devices, from_back(): return lax.ppermute(x, axis, [(i, (i + back) % size) for i in range(size)])  21.4 us
    ppermute x17, waiting for transfers between devices, from_back(): return lax.ppermute(x, axis, [(i, (i + back) % size) for i in range(size)])  20.2 us
    pallas_call x1, Pallas kernels, attend(): pl.pallas_call(attend_kernel, out_shape=jax.ShapeDtypeStruct((NZ * NG, CH...  12.5 us
    unnamed x23, local copies, waits for them, and re-layouts  8.92 us
    all_to_all x1, starting transfers between devices, on_device(): lax.all_to_all(pack(span_qkv), GROUPS, split_axis=0, concat_axis=0, tiled...  5.79 us
    all_to_all x1, waiting for transfers between devices, on_device(): lax.all_to_all(pack(span_qkv), GROUPS, split_axis=0, concat_axis=0, tiled...  3.41 us
  transfers between devices with their start and end apart: 18, of which 8 were waited for; matrix products, arithmetic and copies ran while one was open for 0% of the time, Pallas kernels for 0%

profile of v1, /device:TPU:8, one launch (start us, length us, event | category | flops | bytes accessed | tf_op | source)
XLA Modules:
  0.0 99.0 jit_solution(17819070878385108575)
XLA Ops:
  0.0 1.1 %copy.3.x_ref = bf16[3,9,5120]{2,1,0:T(8,128)(2,1)S(1)} copy(bf16[3,9,5120]{2,0,1:T(4,128)(2,1)} %param.2) | data formatting | bytes 552960 | tf_op args[0]
  1.1 0.9 shard_map.28
  2.0 5.8 %all-to-all-start = ((bf16[8,32,640]{2,1,0:T(8,128)(2,1)}), bf16[8,32,640]{2,1,0:T(8,128)(2,1)S(1)}, u32[]{:S(2)}, u32[]{:S(2)}) async-start(bf16[8,32,640]{2,1,0:T(8,128)(2,1)} %shard_map.28), calls=%async_computation | async-start | bytes 655360 | tf_op jit(solution)/shard_map/all_to_all | solution.py:244
  7.8 2.4 %collective-permute-start.6 = (bf16[2,192,640]{2,1,0:T(8,128)(2,1)S(1)}, bf16[2,192,640]{2,1,0:T(8,128)(2,1)S(1)}, u32[]{:S(2)}, u32[]{:S(2)}) collective-permute-start(bf16[2,192,640]{2,1,0:T(8,128)(2,1)S(1)} %copy-done), channel_id=1, source_target_pairs={{0,32},{16,48},{32,0},{48,16},{1,33},{17,49},{33,1},{49,17},{2,34}... | collective-permute-start | bytes 1474568 | tf_op jit(solution)/shard_map/ppermute | solution.py:235
  10.2 2.0 %collective-permute-start.8 = (bf16[2,192,640]{2,1,0:T(8,128)(2,1)S(1)}, bf16[2,192,640]{2,1,0:T(8,128)(2,1)S(1)}, u32[]{:S(2)}, u32[]{:S(2)}) collective-permute-start(bf16[2,192,640]{2,1,0:T(8,128)(2,1)S(1)} %copy-done), channel_id=1, source_target_pairs={{0,48},{16,0},{32,16},{48,32},{1,49},{17,1},{33,17},{49,33},{2,50}... | collective-permute-start | bytes 1474568 | tf_op jit(solution)/shard_map/ppermute | solution.py:235
  12.2 3.4 %all-to-all-done.x_ref = bf16[8,32,640]{2,1,0:T(8,128)(2,1)S(1)} async-done(((bf16[8,32,640]{2,1,0:T(8,128)(2,1)}), bf16[8,32,640]{2,1,0:T(8,128)(2,1)S(1)}, u32[]{:S(2)}, u32[]{:S(2)}) %all-to-all-start) | async-done | bytes 327712 | tf_op jit(solution)/shard_map/all_to_all | solution.py:244
  15.7 5.5 %collective-permute-start.2 = (bf16[80,640]{1,0:T(8,128)(2,1)S(1)}, bf16[80,640]{1,0:T(8,128)(2,1)S(1)}, u32[]{:S(2)}, u32[]{:S(2)}) collective-permute-start(bf16[80,640]{1,0:T(8,128)(2,1)S(1)} %get-tuple-element.7.refs_0_), channel_id=1, source_target_pairs={{0,192},{64,0},{128,64},{192,128},{1,193},{65,1},{129,65},{193,129... | collective-permute-start | bytes 307208 | tf_op jit(solution)/shard_map/ppermute | solution.py:235
  21.2 2.4 %collective-permute-done.6.refs_8_ = bf16[2,192,640]{2,1,0:T(8,128)(2,1)S(1)} collective-permute-done((bf16[2,192,640]{2,1,0:T(8,128)(2,1)S(1)}, bf16[2,192,640]{2,1,0:T(8,128)(2,1)S(1)}, u32[]{:S(2)}, u32[]{:S(2)}) %collective-permute-start.6) | collective-permute-done | bytes 491552 | tf_op jit(solution)/shard_map/ppermute | solution.py:235
  24.0 8.7 %collective-permute-done.4.refs_6_ = bf16[2,192,640]{2,1,0:T(8,128)(2,1)S(1)} collective-permute-done((bf16[2,192,640]{2,1,0:T(8,128)(2,1)S(1)}, bf16[2,192,640]{2,1,0:T(8,128)(2,1)S(1)}, u32[]{:S(2)}, u32[]{:S(2)}) %collective-permute-start.4) | collective-permute-done | bytes 491552 | tf_op jit(solution)/shard_map/ppermute | solution.py:235
  32.8 1.8 %collective-permute-start.11 = (bf16[2,80,640]{2,1,0:T(8,128)(2,1)S(1)}, bf16[2,80,640]{2,1,0:T(8,128)(2,1)}, u32[]{:S(2)}, u32[]{:S(2)}) collective-permute-start(bf16[2,80,640]{2,1,0:T(8,128)(2,1)S(1)} %get-tuple-element.8.refs_12_), channel_id=1, source_target_pairs={{0,16},{16,32},{32,48},{48,0},{1,17},{17,33},{33,49},{49,1},{2,18}... | collective-permute-start | bytes 614408 | tf_op jit(solution)/shard_map/ppermute | solution.py:235
  34.5 6.3 %collective-permute-start.1 = (bf16[80,640]{1,0:T(8,128)(2,1)S(1)}, bf16[80,640]{1,0:T(8,128)(2,1)S(1)}, u32[]{:S(2)}, u32[]{:S(2)}) collective-permute-start(bf16[80,640]{1,0:T(8,128)(2,1)S(1)} %get-tuple-element.7.refs_0_), channel_id=1, source_target_pairs={{0,128},{64,192},{128,0},{192,64},{1,129},{65,193},{129,1},{193,65... | collective-permute-start | bytes 307208 | tf_op jit(solution)/shard_map/ppermute | solution.py:235
  40.8 1.5 %collective-permute-start = (bf16[80,640]{1,0:T(8,128)(2,1)S(1)}, bf16[80,640]{1,0:T(8,128)(2,1)S(1)}, u32[]{:S(2)}, u32[]{:S(2)}) collective-permute-start(bf16[80,640]{1,0:T(8,128)(2,1)S(1)} %get-tuple-element.7.refs_0_), channel_id=1, source_target_pairs={{0,64},{64,128},{128,192},{192,0},{1,65},{65,129},{129,193},{193,1... | collective-permute-start | bytes 307208 | tf_op jit(solution)/shard_map/ppermute | solution.py:235
  42.9 3.5 %collective-permute-done.1.refs_2_ = bf16[80,640]{1,0:T(8,128)(2,1)S(1)} collective-permute-done((bf16[80,640]{1,0:T(8,128)(2,1)S(1)}, bf16[80,640]{1,0:T(8,128)(2,1)S(1)}, u32[]{:S(2)}, u32[]{:S(2)}) %collective-permute-start.1) | collective-permute-done | bytes 102432 | tf_op jit(solution)/shard_map/ppermute | solution.py:235
  47.0 2.8 %collective-permute-done.refs_1_ = bf16[80,640]{1,0:T(8,128)(2,1)S(1)} collective-permute-done((bf16[80,640]{1,0:T(8,128)(2,1)S(1)}, bf16[80,640]{1,0:T(8,128)(2,1)S(1)}, u32[]{:S(2)}, u32[]{:S(2)}) %collective-permute-start) | collective-permute-done | bytes 102432 | tf_op jit(solution)/shard_map/ppermute | solution.py:235
  51.5 1.4 %collective-permute-done.10.refs_13_ = bf16[2,80,640]{2,1,0:T(8,128)(2,1)S(1)} collective-permute-done((bf16[2,80,640]{2,1,0:T(8,128)(2,1)S(1)}, bf16[2,80,640]{2,1,0:T(8,128)(2,1)S(1)}, u32[]{:S(2)}, u32[]{:S(2)}) %collective-permute-start.10) | collective-permute-done | bytes 204832 | tf_op jit(solution)/shard_map/ppermute | solution.py:235
  55.4 0.8 collective-permute-done.12.refs_15_
  56.3 0.9 copy-done.2
  57.2 0.9 copy-done.4
  58.1 0.9 copy-done.6
  59.0 0.9 copy-done.8
  59.9 0.9 copy-done.10
  60.8 12.5 %shard_map.30 = bf16[32,48,128]{2,1,0:T(8,128)(2,1)S(1)} custom-call(s32[3]{0:T(128)S(1)} %pad_add_fusion.place, bf16[80,640]{1,0:T(8,128)(2,1)S(1)} %copy-done.6, bf16[80,640]{1,0:T(8,128)(2,1)S(1)} %copy-done.10, bf16[80,640]{1,0:T(8,128)(2,1)S(1)} %copy-done.8, bf16[80,640]{1,0:T(8,128)(2,1)S(1)} %collective-permute-done.2.refs_3_, ...), custom_call_target="tpu_custom_call" | custom-call | flops 1782579200 | bytes 5570560 | tf_op jit(solution)/shard_map/pallas_call | solution.py:175
  73.3 24.7 %all_to_all.10.x_ref = bf16[32,48,128]{2,1,0:T(8,128)(2,1)S(1)} all-to-all(bf16[32,48,128]{2,1,0:T(8,128)(2,1)S(1)} %shard_map.30), channel_id=1, replica_groups=mesh['zh'=4,'y'=4,'c'=2,'zl'=2,'x'=4] {'zh','zl','x'}, dimensions={0} | all-to-all | bytes 786432 | tf_op jit(solution)/shard_map/all_to_all | solution.py:252
  98.0 1.0 %shard_map.31 = bf16[9,5120]{1,0:T(8,128)(2,1)} custom-call(bf16[32,48,128]{2,1,0:T(8,128)(2,1)S(1)} %all_to_all.10.x_ref), custom_call_target="tpu_custom_call" | custom-call | tf_op jit(solution)/shard_map/pallas_call | solution.py:224
  (41 shorter events, 6.0 us)
Async XLA Ops:
  2.0 5.8 %copy-start = (bf16[2,192,640]{2,1,0:T(8,128)(2,1)S(1)}, bf16[2,192,640]{2,1,0:T(8,128)(2,1)}, u32[]{:S(2)}) copy-start(bf16[2,192,640]{2,1,0:T(8,128)(2,1)} %refs_4_.1) | copy-start | bytes 1474564
  2.0 13.6 %all-to-all-start = ((bf16[8,32,640]{2,1,0:T(8,128)(2,1)}), bf16[8,32,640]{2,1,0:T(8,128)(2,1)S(1)}, u32[]{:S(2)}, u32[]{:S(2)}) async-start(bf16[8,32,640]{2,1,0:T(8,128)(2,1)} %shard_map.28), calls=%async_computation | async-start | bytes 655360 | tf_op jit(solution)/shard_map/all_to_all | solution.py:244
  7.8 15.8 %collective-permute-start.6 = (bf16[2,192,640]{2,1,0:T(8,128)(2,1)S(1)}, bf16[2,192,640]{2,1,0:T(8,128)(2,1)S(1)}, u32[]{:S(2)}, u32[]{:S(2)}) collective-permute-start(bf16[2,192,640]{2,1,0:T(8,128)(2,1)S(1)} %copy-done), channel_id=1, source_target_pairs={{0,32},{16,48},{32,0},{48,16},{1,33},{17,49},{33,1},{49,17},{2,34}... | collective-permute-start | bytes 1474568 | tf_op jit(solution)/shard_map/ppermute | solution.py:235
  10.2 22.6 %collective-permute-start.4 = (bf16[2,192,640]{2,1,0:T(8,128)(2,1)S(1)}, bf16[2,192,640]{2,1,0:T(8,128)(2,1)S(1)}, u32[]{:S(2)}, u32[]{:S(2)}) collective-permute-start(bf16[2,192,640]{2,1,0:T(8,128)(2,1)S(1)} %copy-done), channel_id=1, source_target_pairs={{0,16},{16,32},{32,48},{48,0},{1,17},{17,33},{33,49},{49,1},{2,18}... | collective-permute-start | bytes 1474568 | tf_op jit(solution)/shard_map/ppermute | solution.py:235
  10.2 22.6 %collective-permute-start.3 = (bf16[2,192,640]{2,1,0:T(8,128)(2,1)S(1)}, bf16[2,192,640]{2,1,0:T(8,128)(2,1)S(1)}, u32[]{:S(2)}, u32[]{:S(2)}) collective-permute-start(bf16[2,192,640]{2,1,0:T(8,128)(2,1)S(1)} %copy-done), channel_id=1, source_target_pairs={{0,8},{8,0},{1,9},{9,1},{2,10},{10,2},{3,11},{11,3},{4,12},{12,4},... | collective-permute-start | bytes 1474568 | tf_op jit(solution)/shard_map/ppermute | solution.py:235
  10.2 24.3 %collective-permute-start.8 = (bf16[2,192,640]{2,1,0:T(8,128)(2,1)S(1)}, bf16[2,192,640]{2,1,0:T(8,128)(2,1)S(1)}, u32[]{:S(2)}, u32[]{:S(2)}) collective-permute-start(bf16[2,192,640]{2,1,0:T(8,128)(2,1)S(1)} %copy-done), channel_id=1, source_target_pairs={{0,48},{16,0},{32,16},{48,32},{1,49},{17,1},{33,17},{49,33},{2,50}... | collective-permute-start | bytes 1474568 | tf_op jit(solution)/shard_map/ppermute | solution.py:235
  15.7 25.1 %collective-permute-start.2 = (bf16[80,640]{1,0:T(8,128)(2,1)S(1)}, bf16[80,640]{1,0:T(8,128)(2,1)S(1)}, u32[]{:S(2)}, u32[]{:S(2)}) collective-permute-start(bf16[80,640]{1,0:T(8,128)(2,1)S(1)} %get-tuple-element.7.refs_0_), channel_id=1, source_target_pairs={{0,192},{64,0},{128,64},{192,128},{1,193},{65,1},{129,65},{193,129... | collective-permute-start | bytes 307208 | tf_op jit(solution)/shard_map/ppermute | solution.py:235
  23.6 26.9 %collective-permute-start.15 = (bf16[2,80,640]{2,1,0:T(8,128)(2,1)S(1)}, bf16[2,80,640]{2,1,0:T(8,128)(2,1)S(1)}, u32[]{:S(2)}, u32[]{:S(2)}) collective-permute-start(bf16[2,80,640]{2,1,0:T(8,128)(2,1)S(1)} %get-tuple-element.8.refs_12_), channel_id=1, source_target_pairs={{0,48},{16,0},{32,16},{48,32},{1,49},{17,1},{33,17},{49,33},{2,50}... | collective-permute-start | bytes 614408 | tf_op jit(solution)/shard_map/ppermute | solution.py:235
  32.8 18.3 %collective-permute-start.13 = (bf16[2,80,640]{2,1,0:T(8,128)(2,1)S(1)}, bf16[2,80,640]{2,1,0:T(8,128)(2,1)}, u32[]{:S(2)}, u32[]{:S(2)}) collective-permute-start(bf16[2,80,640]{2,1,0:T(8,128)(2,1)S(1)} %get-tuple-element.8.refs_12_), channel_id=1, source_target_pairs={{0,32},{16,48},{32,0},{48,16},{1,33},{17,49},{33,1},{49,17},{2,34}... | collective-permute-start | bytes 614408 | tf_op jit(solution)/shard_map/ppermute | solution.py:235
  32.8 18.4 %collective-permute-start.11 = (bf16[2,80,640]{2,1,0:T(8,128)(2,1)S(1)}, bf16[2,80,640]{2,1,0:T(8,128)(2,1)}, u32[]{:S(2)}, u32[]{:S(2)}) collective-permute-start(bf16[2,80,640]{2,1,0:T(8,128)(2,1)S(1)} %get-tuple-element.8.refs_12_), channel_id=1, source_target_pairs={{0,16},{16,32},{32,48},{48,0},{1,17},{17,33},{33,49},{49,1},{2,18}... | collective-permute-start | bytes 614408 | tf_op jit(solution)/shard_map/ppermute | solution.py:235
  34.5 11.9 %collective-permute-start.1 = (bf16[80,640]{1,0:T(8,128)(2,1)S(1)}, bf16[80,640]{1,0:T(8,128)(2,1)S(1)}, u32[]{:S(2)}, u32[]{:S(2)}) collective-permute-start(bf16[80,640]{1,0:T(8,128)(2,1)S(1)} %get-tuple-element.7.refs_0_), channel_id=1, source_target_pairs={{0,128},{64,192},{128,0},{192,64},{1,129},{65,193},{129,1},{193,65... | collective-permute-start | bytes 307208 | tf_op jit(solution)/shard_map/ppermute | solution.py:235
  40.8 9.0 %collective-permute-start = (bf16[80,640]{1,0:T(8,128)(2,1)S(1)}, bf16[80,640]{1,0:T(8,128)(2,1)S(1)}, u32[]{:S(2)}, u32[]{:S(2)}) collective-permute-start(bf16[80,640]{1,0:T(8,128)(2,1)S(1)} %get-tuple-element.7.refs_0_), channel_id=1, source_target_pairs={{0,64},{64,128},{128,192},{192,0},{1,65},{65,129},{129,193},{193,1... | collective-permute-start | bytes 307208 | tf_op jit(solution)/shard_map/ppermute | solution.py:235
  47.0 9.2 %collective-permute-start.7 = (bf16[2,192,640]{2,1,0:T(8,128)(2,1)S(1)}, bf16[2,192,640]{2,1,0:T(8,128)(2,1)S(1)}, u32[]{:S(2)}, u32[]{:S(2)}) collective-permute-start(bf16[2,192,640]{2,1,0:T(8,128)(2,1)S(1)} %collective-permute-done.6.refs_8_), channel_id=1, source_target_pairs={{0,8},{8,0},{1,9},{9,1},{2,10},{10,2},{3,11},{11,3},{4,12},{12,4},... | collective-permute-start | bytes 1474568 | tf_op jit(solution)/shard_map/ppermute | solution.py:235
  50.5 5.7 %collective-permute-start.5 = (bf16[2,192,640]{2,1,0:T(8,128)(2,1)S(1)}, bf16[2,192,640]{2,1,0:T(8,128)(2,1)}, u32[]{:S(2)}, u32[]{:S(2)}) collective-permute-start(bf16[2,192,640]{2,1,0:T(8,128)(2,1)S(1)} %collective-permute-done.4.refs_6_), channel_id=1, source_target_pairs={{0,8},{8,0},{1,9},{9,1},{2,10},{10,2},{3,11},{11,3},{4,12},{12,4},... | collective-permute-start | bytes 1474568 | tf_op jit(solution)/shard_map/ppermute | solution.py:235
  50.5 5.7 %collective-permute-start.9 = (bf16[2,192,640]{2,1,0:T(8,128)(2,1)S(1)}, bf16[2,192,640]{2,1,0:T(8,128)(2,1)}, u32[]{:S(2)}, u32[]{:S(2)}) collective-permute-start(bf16[2,192,640]{2,1,0:T(8,128)(2,1)S(1)} %collective-permute-done.8.refs_10_), channel_id=1, source_target_pairs={{0,8},{8,0},{1,9},{9,1},{2,10},{10,2},{3,11},{11,3},{4,12},{12,4},... | collective-permute-start | bytes 1474568 | tf_op jit(solution)/shard_map/ppermute | solution.py:235
  51.0 1.9 %collective-permute-start.10 = (bf16[2,80,640]{2,1,0:T(8,128)(2,1)S(1)}, bf16[2,80,640]{2,1,0:T(8,128)(2,1)S(1)}, u32[]{:S(2)}, u32[]{:S(2)}) collective-permute-start(bf16[2,80,640]{2,1,0:T(8,128)(2,1)S(1)} %get-tuple-element.8.refs_12_), channel_id=1, source_target_pairs={{0,8},{8,0},{1,9},{9,1},{2,10},{10,2},{3,11},{11,3},{4,12},{12,4},... | collective-permute-start | bytes 614408 | tf_op jit(solution)/shard_map/ppermute | solution.py:235
  51.1 2.7 %collective-permute-start.16 = (bf16[2,80,640]{2,1,0:T(8,128)(2,1)S(1)}, bf16[2,80,640]{2,1,0:T(8,128)(2,1)S(1)}, u32[]{:S(2)}, u32[]{:S(2)}) collective-permute-start(bf16[2,80,640]{2,1,0:T(8,128)(2,1)S(1)} %collective-permute-done.15.refs_18_), channel_id=1, source_target_pairs={{0,8},{8,0},{1,9},{9,1},{2,10},{10,2},{3,11},{11,3},{4,12},{12,4},... | collective-permute-start | bytes 614408 | tf_op jit(solution)/shard_map/ppermute | solution.py:235
  53.6 1.8 %collective-permute-start.14 = (bf16[2,80,640]{2,1,0:T(8,128)(2,1)}, bf16[2,80,640]{2,1,0:T(8,128)(2,1)}, u32[]{:S(2)}, u32[]{:S(2)}) collective-permute-start(bf16[2,80,640]{2,1,0:T(8,128)(2,1)} %collective-permute-done.13.refs_16_), channel_id=1, source_target_pairs={{0,8},{8,0},{1,9},{9,1},{2,10},{10,2},{3,11},{11,3},{4,12},{12,4},... | collective-permute-start | bytes 614408 | tf_op jit(solution)/shard_map/ppermute | solution.py:235
  54.4 1.8 %collective-permute-start.12 = (bf16[2,80,640]{2,1,0:T(8,128)(2,1)}, bf16[2,80,640]{2,1,0:T(8,128)(2,1)}, u32[]{:S(2)}, u32[]{:S(2)}) collective-permute-start(bf16[2,80,640]{2,1,0:T(8,128)(2,1)} %collective-permute-done.11.refs_14_), channel_id=1, source_target_pairs={{0,8},{8,0},{1,9},{9,1},{2,10},{10,2},{3,11},{11,3},{4,12},{12,4},... | collective-permute-start | bytes 614408 | tf_op jit(solution)/shard_map/ppermute | solution.py:235
  56.3 0.9 copy-start.2
  57.2 0.9 copy-start.4
  58.1 0.9 copy-start.6
  59.0 0.9 copy-start.8
  59.9 0.9 copy-start.10
  (5 other events, 3.3 us)

commit v2 on v0

v2 whole, which is shorter than its diff:
```python
import math

import jax
import jax.numpy as jnp
from jax import lax
from jax.experimental import pallas as pl
from jax.experimental.pallas import tpu as pltpu
from jax.sharding import Mesh, PartitionSpec as P

HEADS = 40
HEAD_DIM = 128
TOKENS = 2304
HIST = 6144
FRAME_LEN = 768

FRAMES = ("zh", "y", "c")
GROUPS = ("zl", "x")
NZ, NY, NC, NG = 4, 4, 2, 8
HERE = HEADS // NG
WIDE = HERE * HEAD_DIM
HOME = TOKENS // (NZ * NY * NC * NG)
OWN = HOME * NG
HKEYS = HIST // (NZ * NY * NC)
NHIST = NY * NC * HKEYS
ROWS = HERE * HOME
CHUNK = 48
KV_CHUNK = 96
CHUNKS = NZ * NG
QROWS = CHUNKS * HOME
SKEYS = NY * NG * HOME
PIECES = 10
SCALE = math.log2(math.e) / math.sqrt(HEAD_DIM)
F32, BF16 = jnp.float32, jnp.bfloat16


def params(mib):
    return pltpu.CompilerParams(vmem_limit_bytes=mib * 2**20)


IN_VMEM = pl.BlockSpec(memory_space=pltpu.VMEM)
IN_SMEM = pl.BlockSpec(memory_space=pltpu.SMEM)
ANYWHERE = pl.BlockSpec(memory_space=pl.ANY)


def pack_kernel(x_ref, q_ref, kv_ref, q_rows, kv_rows):
    for g in range(NG):
        q_rows[g, ROWS:, :] = jnp.zeros((CHUNK - ROWS, HEAD_DIM), F32)
        kv_rows[g, 2 * ROWS :, :] = jnp.zeros((KV_CHUNK - 2 * ROWS, HEAD_DIM), F32)
        for e in range(HERE):
            cols = slice((g * HERE + e) * HEAD_DIM, (g * HERE + e + 1) * HEAD_DIM)
            low = e * HOME
            q_rows[g, low : low + HOME, :] = x_ref[0, :, cols].astype(F32)
            kv_rows[g, low : low + HOME, :] = x_ref[1, :, cols].astype(F32)
            low += ROWS
            kv_rows[g, low : low + HOME, :] = x_ref[2, :, cols].astype(F32)
        q = q_rows[g].astype(BF16)
        for z in range(NZ):
            q_ref[z * NG + g] = q
        kv_ref[g] = kv_rows[g].astype(BF16)


def pack(x):
    return pl.pallas_call(
        pack_kernel,
        out_shape=(
            jax.ShapeDtypeStruct((NZ * NG, CHUNK, HEAD_DIM), BF16),
            jax.ShapeDtypeStruct((NG, KV_CHUNK, HEAD_DIM), BF16),
        ),
        in_specs=[IN_VMEM],
        out_specs=(IN_VMEM, IN_VMEM),
        scratch_shapes=[
            pltpu.VMEM((NG, CHUNK, HEAD_DIM), F32),
            pltpu.VMEM((NG, KV_CHUNK, HEAD_DIM), F32),
        ],
        compiler_params=params(8),
    )(x)


def after_kernel(x_ref, *refs):
    refs[-1][...] = x_ref[...]


def after(x, *others):
    return pl.pallas_call(
        after_kernel,
        out_shape=jax.ShapeDtypeStruct(x.shape, x.dtype),
        in_specs=[IN_VMEM] + [ANYWHERE] * len(others),
        out_specs=IN_VMEM,
        compiler_params=params(8),
    )(x, *others)


def sort_kernel(*refs):
    o_ref, chunks, rows, sems = refs[-4:]
    copies = []
    for n in range(NY):
        where = chunks.at[pl.ds(n * NG, NG)]
        copies.append(pltpu.make_async_copy(refs[n], where, sems.at[n]))
    for copy in copies:
        copy.start()
    for copy in copies:
        copy.wait()
    rows[...] = chunks[...].astype(F32).reshape(CHUNKS * KV_CHUNK, HEAD_DIM)
    for i in range(2):
        for e in range(HERE):
            for t in range(HOME):
                row = (i * HERE + e) * HOME + t
                o_ref[i, e, t * CHUNKS : (t + 1) * CHUNKS, :] = rows[
                    pl.ds(row, CHUNKS, stride=KV_CHUNK), :
                ].astype(BF16)


def sort_span(span, *after):
    return pl.pallas_call(
        sort_kernel,
        out_shape=jax.ShapeDtypeStruct((2, HERE, SKEYS, HEAD_DIM), BF16),
        in_specs=[ANYWHERE] * (NY + len(after)),
        out_specs=IN_VMEM,
        scratch_shapes=[
            pltpu.VMEM((CHUNKS, KV_CHUNK, HEAD_DIM), BF16),
            pltpu.VMEM((CHUNKS * KV_CHUNK, HEAD_DIM), F32),
            pltpu.SemaphoreType.DMA((NY,)),
        ],
        compiler_params=params(8),
        cost_estimate=pl.CostEstimate(flops=0, bytes_accessed=0, transcendentals=0),
    )(*span, *after)


def sort_queries_kernel(x_ref, o_ref, rows):
    rows[...] = x_ref[...].astype(F32).reshape(CHUNKS * CHUNK, HEAD_DIM)
    for e in range(HERE):
        for t in range(HOME):
            row = e * HOME + t
            o_ref[e, t * CHUNKS : (t + 1) * CHUNKS, :] = rows[
                pl.ds(row, CHUNKS, stride=CHUNK), :
            ].astype(BF16)


def sort_queries(x):
    return pl.pallas_call(
        sort_queries_kernel,
        out_shape=jax.ShapeDtypeStruct((HERE, QROWS, HEAD_DIM), BF16),
        in_specs=[IN_VMEM],
        out_specs=IN_VMEM,
        scratch_shapes=[pltpu.VMEM((CHUNKS * CHUNK, HEAD_DIM), F32)],
        compiler_params=params(8),
    )(x)


def keys_and_values(refs):
    whole = [(refs[n].at[0], refs[n].at[1]) for n in range(6)]
    return whole + [(refs[6], refs[8]), (refs[7], refs[9])]


def against(queries, keys):
    return lax.dot_general(
        queries, keys, (((1,), (1,)), ((), ())), preferred_element_type=F32
    )


def attend_kernel(place, q_ref, own_span, other_span, *refs):
    hist = keys_and_values(refs[:PIECES])
    o_ref, q_all, rows, kv_span, k_hist, v_hist, sums, tops, totals = refs[PIECES : PIECES + 9]
    q_sem, span_sems, sems = refs[PIECES + 9 :]
    zh, y, c = place[0], place[1], place[2]
    early, late = [], []
    early.append(pltpu.make_async_copy(q_ref, q_all, q_sem.at[0]))
    for b, source in enumerate((own_span, other_span)):
        where = kv_span.at[:, :, pl.ds(b * SKEYS, SKEYS)]
        early.append(pltpu.make_async_copy(source, where, span_sems.at[b]))
    for n, (keys, values) in enumerate(hist):
        where = pl.ds(n * HKEYS, HKEYS)
        late.append(pltpu.make_async_copy(keys, k_hist.at[where], sems.at[0, n]))
        late.append(pltpu.make_async_copy(values, v_hist.at[where], sems.at[1, n]))
    for copy in early + late:
        copy.start()

    row = lax.broadcasted_iota(jnp.int32, (QROWS, 1), 0)
    sender = lax.rem(row, CHUNKS)
    index = ((sender // NG) * NY + y) * NC + c
    q_token = index * OWN + lax.rem(sender, NG) * HOME + row // CHUNKS
    q_frame = q_token // FRAME_LEN
    col = lax.broadcasted_iota(jnp.int32, (1, NC * SKEYS), 1)
    core = jnp.where(col < SKEYS, c, 1 - c)
    col = lax.rem(col, SKEYS)
    sender = lax.rem(col, CHUNKS)
    index = (zh * NY + lax.rem(y + NY - sender // NG, NY)) * NC + core
    k_token = index * OWN + lax.rem(sender, NG) * HOME + col // CHUNKS
    allowed = q_frame >= k_token // FRAME_LEN

    for copy in early:
        copy.wait()
    for e in range(HERE):
        score = jnp.where(allowed, against(q_all[e], kv_span[0, e]), -1e30)
        top = jnp.max(score, axis=1, keepdims=True)
        weight = jnp.exp2((score - top) * SCALE)
        tops[e] = jnp.broadcast_to(top, (QROWS, HEAD_DIM))
        totals[e] = jnp.broadcast_to(
            jnp.sum(weight, axis=1, keepdims=True), (QROWS, HEAD_DIM)
        )
        sums[e] = jnp.dot(weight.astype(BF16), kv_span[1, e], preferred_element_type=F32)
    for copy in late:
        copy.wait()
    lane = lax.broadcasted_iota(jnp.int32, (CHUNKS, HEAD_DIM), 1)
    lses = jnp.zeros((CHUNKS, HEAD_DIM), F32)
    for e in range(HERE):
        cols = slice(e * HEAD_DIM, (e + 1) * HEAD_DIM)
        score = against(q_all[e], k_hist[:, cols])
        before = tops[e]
        top = jnp.maximum(before, jnp.max(score, axis=1, keepdims=True))
        factor = jnp.exp2((before - top) * SCALE)
        weight = jnp.exp2((score - top[:, :1]) * SCALE)
        total = totals[e] * factor + jnp.sum(weight, axis=1, keepdims=True)
        summed = sums[e] * factor + jnp.dot(
            weight.astype(BF16), v_hist[:, cols], preferred_element_type=F32
        )
        partial = summed / total
        lse = top * SCALE + jnp.log2(total)
        for t in range(HOME):
            here = slice(t * CHUNKS, (t + 1) * CHUNKS)
            row = e * HOME + t
            rows[pl.ds(row, CHUNKS, stride=CHUNK), :] = partial[here]
            lses = jnp.where(lane == row, lse[here], lses)

    high = lses.astype(BF16).astype(F32)
    middle = (lses - high).astype(BF16).astype(F32)
    for n, term in enumerate((high, middle, lses - high - middle)):
        rows[pl.ds(ROWS + n, CHUNKS, stride=CHUNK), :] = term
    o_ref[...] = rows[...].reshape(CHUNKS, CHUNK, HEAD_DIM).astype(BF16)


def attend(place, q, own_span, other_span, hist):
    keys = NHIST + NC * SKEYS
    by_head = pltpu.VMEM((HERE, QROWS, HEAD_DIM), F32)
    return pl.pallas_call(
        attend_kernel,
        out_shape=jax.ShapeDtypeStruct((CHUNKS, CHUNK, HEAD_DIM), BF16),
        in_specs=[IN_SMEM] + [ANYWHERE] * (3 + PIECES),
        out_specs=IN_VMEM,
        scratch_shapes=[
            pltpu.VMEM((HERE, QROWS, HEAD_DIM), BF16),
            pltpu.VMEM((CHUNKS * CHUNK, HEAD_DIM), F32),
            pltpu.VMEM((2, HERE, NC * SKEYS, HEAD_DIM), BF16),
            pltpu.VMEM((NHIST, WIDE), BF16),
            pltpu.VMEM((NHIST, WIDE), BF16),
            by_head,
            by_head,
            by_head,
            pltpu.SemaphoreType.DMA((1,)),
            pltpu.SemaphoreType.DMA((NC,)),
            pltpu.SemaphoreType.DMA((2, NY * NC)),
        ],
        compiler_params=params(24),
        cost_estimate=pl.CostEstimate(
            flops=4 * QROWS * keys * WIDE,
            bytes_accessed=4 * keys * WIDE,
            transcendentals=QROWS * keys * HERE,
        ),
    )(place, q, own_span, other_span, *hist)


def merge_kernel(x_ref, o_ref, rows):
    eye = lax.broadcasted_iota(jnp.int32, (CHUNK, HEAD_DIM), 0) == lax.broadcasted_iota(
        jnp.int32, (CHUNK, HEAD_DIM), 1
    )
    for g in range(NG):
        parts = [x_ref[z * NG + g].astype(F32) for z in range(NZ)]
        lses = [
            (p[ROWS : ROWS + 1] + p[ROWS + 1 : ROWS + 2]) + p[ROWS + 2 : ROWS + 3] for p in parts
        ]
        top = jnp.maximum(jnp.maximum(lses[0], lses[1]), jnp.maximum(lses[2], lses[3]))
        weights = [jnp.exp2(v - top) for v in lses]
        total = (weights[0] + weights[1]) + (weights[2] + weights[3])
        out = jnp.zeros((CHUNK, HEAD_DIM), F32)
        for p, w in zip(parts, weights):
            share = jnp.sum(jnp.where(eye, w / total, 0.0), axis=1, keepdims=True)
            out = out + share * p
        rows[g] = out
        for e in range(HERE):
            low = (g * HERE + e) * HEAD_DIM
            o_ref[:, low : low + HEAD_DIM] = rows[g, e * HOME : (e + 1) * HOME, :].astype(BF16)


def merge(x):
    return pl.pallas_call(
        merge_kernel,
        out_shape=jax.ShapeDtypeStruct((HOME, HEADS * HEAD_DIM), BF16),
        in_specs=[IN_VMEM],
        out_specs=IN_VMEM,
        scratch_shapes=[pltpu.VMEM((NG, CHUNK, HEAD_DIM), F32)],
        compiler_params=params(8),
    )(x)


def from_back(x, axis, size, back):
    return lax.ppermute(x, axis, [(i, (i + back) % size) for i in range(size)])


def exchange(x, axes):
    return lax.all_to_all(x, axes, split_axis=0, concat_axis=0, tiled=True)


def on_device(span_qkv, history_kv):
    place = jnp.stack([lax.axis_index(a) for a in FRAMES]).astype(jnp.int32)
    other = lambda x: from_back(x, "c", NC, 1)
    back = from_back(history_kv, "y", NY, 1)
    ahead = from_back(history_kv, "y", NY, NY - 1)
    near = [history_kv, other(history_kv), back, other(back), ahead, other(ahead)]
    keys = from_back(back[0], "y", NY, 1)
    values = from_back(ahead[1], "y", NY, NY - 1)
    hist = near + [keys, other(keys), values, other(values)]

    q, kv = pack(span_qkv)
    kv = after(exchange(kv, GROUPS), back, ahead)
    q = exchange(q, ("zh",) + GROUPS)
    span = sort_span([kv] + [from_back(kv, "y", NY, d) for d in range(1, NY)], keys, values)
    partial = attend(place, sort_queries(q), span, other(span), hist)
    return merge(exchange(partial, ("zh",) + GROUPS))


def solution(mesh):
    cut = Mesh(mesh.devices.reshape(NZ, NY, NC, 2, 4), FRAMES + GROUPS)
    in_specs = (P(None, FRAMES + GROUPS, None), P(None, FRAMES, GROUPS))
    out_specs = P(FRAMES + GROUPS, None)
    return jax.shard_map(
        on_device, mesh=cut, in_specs=in_specs, out_specs=out_specs, check_vma=False
    )
```

time: 301 us -> 78.3 us (0.26)
  waiting for transfers between devices: 137 us -> 13.9 us
  local copies, waits for them, and re-layouts: 55.7 us -> 2.7 us
  matrix products: 42 us -> 0 us
  starting transfers between devices: 0.04 us -> 28.7 us
  blocking collectives: 37.9 us -> 17.6 us
  Pallas kernels: 0 us -> 14.7 us
  between operations: 13.8 us -> 0.14 us
  other arithmetic: 12.6 us -> 0.08 us
    all_gather x2 -> x0, waiting for transfers between devices: 136 us -> none  [the longest x1 70.2 us: on_device(): lax.all_gather(history_kv, 'frames', axis=1, tiled=True)]
    dot_general x20 -> x0, matrix products: 42 us -> none  [the longest x10 24.7 us: head_scores(): jnp.einsum('qd,kd->qk', queries, keys, preferred_element_type=jnp.float32)]
    all_to_all x2 -> x1, blocking collectives: 37.9 us -> 17.6 us  [exchange(): return lax.all_to_all(x, axes, split_axis=0, concat_axis=0, tiled=True)]
    unnamed x41 -> x5, local copies, waits for them, and re-layouts: 21.1 us -> 2.65 us
    all_to_all x0 -> x2, starting transfers between devices: none -> 16.7 us  [exchange(): return lax.all_to_all(x, axes, split_axis=0, concat_axis=0, tiled=True)]
    pallas_call x0 -> x6, Pallas kernels: none -> 14.7 us  [the longest x1 10.5 us: attend(): pl.pallas_call(attend_kernel, out_shape=jax.ShapeDtypeStruct((CHUNKS, CHU...]
    slice x3 -> x0, local copies, waits for them, and re-layouts: 13.6 us -> none  [the longest x1 12.2 us: fold_heads(): piece[1][:, low:high]]
    ppermute x0 -> x13, starting transfers between devices: none -> 12 us  [from_back(): return lax.ppermute(x, axis, [(i, (i + back) % size) for i in range(size)])]
  transfers between devices with their start and end apart: 2 -> 15, of which waited for: 2 -> 4; matrix products, arithmetic and copies ran while one was open for 11% -> 2% of each run, Pallas kernels for 0% -> 4%
where the time goes in v2:
time: 78.3 us; the launch traced here: 77.9 us
  starting transfers between devices  28.7 us (37%)
  blocking collectives  17.6 us (22%)
  Pallas kernels  14.7 us (19%)
  waiting for transfers between devices  13.9 us (18%)
  local copies, waits for them, and re-layouts  2.7 us (3%)
    all_to_all x1, blocking collectives, exchange(): return lax.all_to_all(x, axes, split_axis=0, concat_axis=0, tiled=True)  17.6 us
    all_to_all x2, starting transfers between devices, exchange(): return lax.all_to_all(x, axes, split_axis=0, concat_axis=0, tiled=True)  16.7 us
    ppermute x13, starting transfers between devices, from_back(): return lax.ppermute(x, axis, [(i, (i + back) % size) for i in range(size)])  12 us
    pallas_call x1, Pallas kernels, attend(): pl.pallas_call(attend_kernel, out_shape=jax.ShapeDtypeStruct((CHUNKS, CHU...  10.5 us
    all_to_all x2, waiting for transfers between devices, exchange(): return lax.all_to_all(x, axes, split_axis=0, concat_axis=0, tiled=True)  10.2 us
    ppermute x13, waiting for transfers between devices, from_back(): return lax.ppermute(x, axis, [(i, (i + back) % size) for i in range(size)])  3.71 us
    unnamed x5, local copies, waits for them, and re-layouts  2.65 us
    pallas_call x1, Pallas kernels, sort_span(): pl.pallas_call(sort_kernel, out_shape=jax.ShapeDtypeStruct((2, HERE, SKEY...  1.96 us
  transfers between devices with their start and end apart: 15, of which 4 were waited for; matrix products, arithmetic and copies ran while one was open for 2% of the time, Pallas kernels for 4%

profile of v2, /device:TPU:8, one launch (start us, length us, event | category | flops | bytes accessed | tf_op | source)
XLA Modules:
  0.0 77.9 jit_solution(1118966884704864227)
XLA Ops:
  0.0 2.2 %collective-permute-start.1 = (bf16[2,192,640]{2,1,0:T(8,128)(2,1)}, bf16[2,192,640]{2,1,0:T(8,128)(2,1)S(1)}, u32[]{:S(2)}, u32[]{:S(2)}) collective-permute-start(bf16[2,192,640]{2,1,0:T(8,128)(2,1)} %refs_0_.1), channel_id=1, source_target_pairs={{0,48},{16,0},{32,16},{48,32},{1,49},{17,1},{33,17},{49,33},{2,50}... | collective-permute-start | bytes 1474568 | tf_op jit(solution)/shard_map/ppermute | solution.py:296
  2.2 1.1 %copy.3.x_ref = bf16[3,9,5120]{2,1,0:T(8,128)(2,1)S(1)} copy(bf16[3,9,5120]{2,0,1:T(4,128)(2,1)} %param.2) | data formatting | bytes 552960 | tf_op args[0]
  3.3 1.0 %shard_map.28 = (bf16[32,48,128]{2,1,0:T(8,128)(2,1)}, bf16[8,96,128]{2,1,0:T(8,128)(2,1)}) custom-call(bf16[3,9,5120]{2,1,0:T(8,128)(2,1)S(1)} %copy.3.x_ref), custom_call_target="tpu_custom_call" | custom-call | tf_op jit(solution)/shard_map/pallas_call | solution.py:63
  4.3 5.5 %all-to-all-start.1 = ((bf16[8,96,128]{2,1,0:T(8,128)(2,1)}), bf16[8,96,128]{2,1,0:T(8,128)(2,1)S(1)}, u32[]{:S(2)}, u32[]{:S(2)}) async-start(bf16[8,96,128]{2,1,0:T(8,128)(2,1)} %get-tuple-element.8), calls=%async_computation.1 | async-start | bytes 393216 | tf_op jit(solution)/shard_map/all_to_all | solution.py:300
  9.8 3.4 %collective-permute-done.1.refs_1_.refs_4_ = bf16[2,192,640]{2,1,0:T(8,128)(2,1)S(1)} collective-permute-done((bf16[2,192,640]{2,1,0:T(8,128)(2,1)}, bf16[2,192,640]{2,1,0:T(8,128)(2,1)S(1)}, u32[]{:S(2)}, u32[]{:S(2)}) %collective-permute-start.1) | collective-permute-done | bytes 491552 | tf_op jit(solution)/shard_map/ppermute | solution.py:296
  13.2 1.2 %collective-permute-start.6 = (bf16[192,640]{1,0:T(8,128)(2,1)S(1)}, bf16[192,640]{1,0:T(8,128)(2,1)S(1)}, u32[]{:S(2)}, u32[]{:S(2)}) collective-permute-start(bf16[192,640]{1,0:T(8,128)(2,1)S(1)} %slice_bitcast_fusion), channel_id=1, source_target_pairs={{0,48},{16,0},{32,16},{48,32},{1,49},{17,1},{33,17},{49,33},{2,50}... | collective-permute-start | bytes 737288 | tf_op jit(solution)/shard_map/ppermute | solution.py:296
  14.4 0.3 collective-permute-done.refs_0_.refs_2_
  14.7 0.7 collective-permute-start.5
  15.4 1.3 %all-to-all-done.1.x_ref = bf16[8,96,128]{2,1,0:T(8,128)(2,1)S(1)} async-done(((bf16[8,96,128]{2,1,0:T(8,128)(2,1)}), bf16[8,96,128]{2,1,0:T(8,128)(2,1)S(1)}, u32[]{:S(2)}, u32[]{:S(2)}) %all-to-all-start.1) | async-done | bytes 196640 | tf_op jit(solution)/shard_map/all_to_all | solution.py:300
  16.7 1.5 %collective-permute-start.4 = (bf16[8,96,128]{2,1,0:T(8,128)(2,1)S(1)}, bf16[8,96,128]{2,1,0:T(8,128)(2,1)S(1)}, u32[]{:S(2)}, u32[]{:S(2)}) collective-permute-start(bf16[8,96,128]{2,1,0:T(8,128)(2,1)S(1)} %shard_map.30.refs_0_), channel_id=1, source_target_pairs={{0,48},{16,0},{32,16},{48,32},{1,49},{17,1},{33,17},{49,33},{2,50}... | collective-permute-start | bytes 589832 | tf_op jit(solution)/shard_map/ppermute | solution.py:296
  18.2 2.2 %collective-permute-start.3 = (bf16[8,96,128]{2,1,0:T(8,128)(2,1)S(1)}, bf16[8,96,128]{2,1,0:T(8,128)(2,1)S(1)}, u32[]{:S(2)}, u32[]{:S(2)}) collective-permute-start(bf16[8,96,128]{2,1,0:T(8,128)(2,1)S(1)} %shard_map.30.refs_0_), channel_id=1, source_target_pairs={{0,32},{16,48},{32,0},{48,16},{1,33},{17,49},{33,1},{49,17},{2,34}... | collective-permute-start | bytes 589832 | tf_op jit(solution)/shard_map/ppermute | solution.py:296
  20.4 2.5 %collective-permute-start.2 = (bf16[8,96,128]{2,1,0:T(8,128)(2,1)S(1)}, bf16[8,96,128]{2,1,0:T(8,128)(2,1)S(1)}, u32[]{:S(2)}, u32[]{:S(2)}) collective-permute-start(bf16[8,96,128]{2,1,0:T(8,128)(2,1)S(1)} %shard_map.30.refs_0_), channel_id=1, source_target_pairs={{0,16},{16,32},{32,48},{48,0},{1,17},{17,33},{33,49},{49,1},{2,18}... | collective-permute-start | bytes 589832 | tf_op jit(solution)/shard_map/ppermute | solution.py:296
  22.9 11.2 %all-to-all-start = ((bf16[32,48,128]{2,1,0:T(8,128)(2,1)}), bf16[32,48,128]{2,1,0:T(8,128)(2,1)S(1)}, u32[]{:S(2)}, u32[]{:S(2)}) async-start(bf16[32,48,128]{2,1,0:T(8,128)(2,1)} %get-tuple-element.7), calls=%async_computation | async-start | bytes 786432 | tf_op jit(solution)/shard_map/all_to_all | solution.py:300
  34.3 2.0 %shard_map.31.own_span = bf16[2,5,288,128]{3,2,1,0:T(8,128)(2,1)S(1)} custom-call(bf16[8,96,128]{2,1,0:T(8,128)(2,1)S(1)} %shard_map.30.refs_0_, bf16[8,96,128]{2,1,0:T(8,128)(2,1)S(1)} %collective-permute-done.2.refs_1_, bf16[8,96,128]{2,1,0:T(8,128)(2,1)S(1)} %collective-permute-done.3.refs_2_, bf16[8,96,128]{2,1,0:T(8,128)(2,1)S(1)} %collective-permute-done.4.refs_3_, ...), custom_call_target="tpu_custom_call" | custom-call | tf_op jit(solution)/shard_map/pallas_call | solution.py:114
  36.3 0.6 collective-permute-start.7
  37.0 0.4 collective-permute-start.9
  37.5 0.8 %copy-done = bf16[2,192,640]{2,1,0:T(8,128)(2,1)} copy-done((bf16[2,192,640]{2,1,0:T(8,128)(2,1)}, bf16[2,192,640]{2,1,0:T(8,128)(2,1)S(1)}, u32[]{:S(2)}) %copy-start) | copy-done | bytes 491544
  38.3 0.4 collective-permute-start.11
  38.8 8.9 %all-to-all-done.x_ref = bf16[32,48,128]{2,1,0:T(8,128)(2,1)S(1)} async-done(((bf16[32,48,128]{2,1,0:T(8,128)(2,1)}), bf16[32,48,128]{2,1,0:T(8,128)(2,1)S(1)}, u32[]{:S(2)}, u32[]{:S(2)}) %all-to-all-start) | async-done | bytes 393248 | tf_op jit(solution)/shard_map/all_to_all | solution.py:300
  47.7 0.3 shard_map.29.q_ref
  48.0 0.7 copy-done.1
  48.7 10.5 %shard_map.32 = bf16[32,48,128]{2,1,0:T(8,128)(2,1)S(1)} custom-call(s32[3]{0:T(128)S(1)} %pad_add_fusion.place, bf16[5,288,128]{2,1,0:T(8,128)(2,1)S(1)} %shard_map.29.q_ref, bf16[2,5,288,128]{3,2,1,0:T(8,128)(2,1)S(1)} %shard_map.31.own_span, bf16[2,5,288,128]{3,2,1,0:T(8,128)(2,1)S(1)} %collective-permute-done.7.other_span, bf16[2,192,640]{2,1,0:T(8,128)(2,1)} %refs_0_.1, ...), custom_call_target="tpu_custom_call" | custom-call | flops 1557135360 | bytes 5406720 | tf_op jit(solution)/shard_map/pallas_call | solution.py:235
  59.2 17.6 %all_to_all.15.x_ref = bf16[32,48,128]{2,1,0:T(8,128)(2,1)S(1)} all-to-all(bf16[32,48,128]{2,1,0:T(8,128)(2,1)S(1)} %shard_map.32), channel_id=1, replica_groups=mesh['zh'=4,'y'=4,'c'=2,'zl'=2,'x'=4] {'zh','zl','x'}, dimensions={0} | all-to-all | bytes 786432 | tf_op jit(solution)/shard_map/all_to_all | solution.py:300
  76.9 1.0 %shard_map.33 = bf16[9,5120]{1,0:T(8,128)(2,1)} custom-call(bf16[32,48,128]{2,1,0:T(8,128)(2,1)S(1)} %all_to_all.15.x_ref), custom_call_target="tpu_custom_call" | custom-call | tf_op jit(solution)/shard_map/pallas_call | solution.py:285
  (21 shorter events, 0.5 us)
Async XLA Ops:
  0.0 13.2 %collective-permute-start.1 = (bf16[2,192,640]{2,1,0:T(8,128)(2,1)}, bf16[2,192,640]{2,1,0:T(8,128)(2,1)S(1)}, u32[]{:S(2)}, u32[]{:S(2)}) collective-permute-start(bf16[2,192,640]{2,1,0:T(8,128)(2,1)} %refs_0_.1), channel_id=1, source_target_pairs={{0,48},{16,0},{32,16},{48,32},{1,49},{17,1},{33,17},{49,33},{2,50}... | collective-permute-start | bytes 1474568 | tf_op jit(solution)/shard_map/ppermute | solution.py:296
  2.2 12.5 %collective-permute-start = (bf16[2,192,640]{2,1,0:T(8,128)(2,1)}, bf16[2,192,640]{2,1,0:T(8,128)(2,1)S(1)}, u32[]{:S(2)}, u32[]{:S(2)}) collective-permute-start(bf16[2,192,640]{2,1,0:T(8,128)(2,1)} %refs_0_.1), channel_id=1, source_target_pairs={{0,16},{16,32},{32,48},{48,0},{1,17},{17,33},{33,49},{49,1},{2,18}... | collective-permute-start | bytes 1474568 | tf_op jit(solution)/shard_map/ppermute | solution.py:296
  4.3 12.4 %all-to-all-start.1 = ((bf16[8,96,128]{2,1,0:T(8,128)(2,1)}), bf16[8,96,128]{2,1,0:T(8,128)(2,1)S(1)}, u32[]{:S(2)}, u32[]{:S(2)}) async-start(bf16[8,96,128]{2,1,0:T(8,128)(2,1)} %get-tuple-element.8), calls=%async_computation.1 | async-start | bytes 393216 | tf_op jit(solution)/shard_map/all_to_all | solution.py:300
  13.2 21.1 %collective-permute-start.6 = (bf16[192,640]{1,0:T(8,128)(2,1)S(1)}, bf16[192,640]{1,0:T(8,128)(2,1)S(1)}, u32[]{:S(2)}, u32[]{:S(2)}) collective-permute-start(bf16[192,640]{1,0:T(8,128)(2,1)S(1)} %slice_bitcast_fusion), channel_id=1, source_target_pairs={{0,48},{16,0},{32,16},{48,32},{1,49},{17,1},{33,17},{49,33},{2,50}... | collective-permute-start | bytes 737288 | tf_op jit(solution)/shard_map/ppermute | solution.py:296
  14.7 19.7 %collective-permute-start.5 = (bf16[192,640]{1,0:T(8,128)(2,1)S(1)}, bf16[192,640]{1,0:T(8,128)(2,1)S(1)}, u32[]{:S(2)}, u32[]{:S(2)}) collective-permute-start(bf16[192,640]{1,0:T(8,128)(2,1)S(1)} %slice_bitcast_fusion.1), channel_id=1, source_target_pairs={{0,16},{16,32},{32,48},{48,0},{1,17},{17,33},{33,49},{49,1},{2,18}... | collective-permute-start | bytes 737288 | tf_op jit(solution)/shard_map/ppermute | solution.py:296
  16.7 17.5 %collective-permute-start.4 = (bf16[8,96,128]{2,1,0:T(8,128)(2,1)S(1)}, bf16[8,96,128]{2,1,0:T(8,128)(2,1)S(1)}, u32[]{:S(2)}, u32[]{:S(2)}) collective-permute-start(bf16[8,96,128]{2,1,0:T(8,128)(2,1)S(1)} %shard_map.30.refs_0_), channel_id=1, source_target_pairs={{0,48},{16,0},{32,16},{48,32},{1,49},{17,1},{33,17},{49,33},{2,50}... | collective-permute-start | bytes 589832 | tf_op jit(solution)/shard_map/ppermute | solution.py:296
  18.2 16.1 %collective-permute-start.3 = (bf16[8,96,128]{2,1,0:T(8,128)(2,1)S(1)}, bf16[8,96,128]{2,1,0:T(8,128)(2,1)S(1)}, u32[]{:S(2)}, u32[]{:S(2)}) collective-permute-start(bf16[8,96,128]{2,1,0:T(8,128)(2,1)S(1)} %shard_map.30.refs_0_), channel_id=1, source_target_pairs={{0,32},{16,48},{32,0},{48,16},{1,33},{17,49},{33,1},{49,17},{2,34}... | collective-permute-start | bytes 589832 | tf_op jit(solution)/shard_map/ppermute | solution.py:296
  20.4 13.9 %collective-permute-start.2 = (bf16[8,96,128]{2,1,0:T(8,128)(2,1)S(1)}, bf16[8,96,128]{2,1,0:T(8,128)(2,1)S(1)}, u32[]{:S(2)}, u32[]{:S(2)}) collective-permute-start(bf16[8,96,128]{2,1,0:T(8,128)(2,1)S(1)} %shard_map.30.refs_0_), channel_id=1, source_target_pairs={{0,16},{16,32},{32,48},{48,0},{1,17},{17,33},{33,49},{49,1},{2,18}... | collective-permute-start | bytes 589832 | tf_op jit(solution)/shard_map/ppermute | solution.py:296
  22.9 24.8 %all-to-all-start = ((bf16[32,48,128]{2,1,0:T(8,128)(2,1)}), bf16[32,48,128]{2,1,0:T(8,128)(2,1)S(1)}, u32[]{:S(2)}, u32[]{:S(2)}) async-start(bf16[32,48,128]{2,1,0:T(8,128)(2,1)} %get-tuple-element.7), calls=%async_computation | async-start | bytes 786432 | tf_op jit(solution)/shard_map/all_to_all | solution.py:300
  34.2 3.3 %collective-permute-start.8 = (bf16[2,192,640]{2,1,0:T(8,128)(2,1)}, bf16[2,192,640]{2,1,0:T(8,128)(2,1)S(1)}, u32[]{:S(2)}, u32[]{:S(2)}) collective-permute-start(bf16[2,192,640]{2,1,0:T(8,128)(2,1)} %refs_0_.1), channel_id=1, source_target_pairs={{0,8},{8,0},{1,9},{9,1},{2,10},{10,2},{3,11},{11,3},{4,12},{12,4},... | collective-permute-start | bytes 1474568 | tf_op jit(solution)/shard_map/ppermute | solution.py:296
  36.3 11.7 %collective-permute-start.7 = (bf16[2,5,288,128]{3,2,1,0:T(8,128)(2,1)S(1)}, bf16[2,5,288,128]{3,2,1,0:T(8,128)(2,1)S(1)}, u32[]{:S(2)}, u32[]{:S(2)}) collective-permute-start(bf16[2,5,288,128]{3,2,1,0:T(8,128)(2,1)S(1)} %shard_map.31.own_span), channel_id=1, source_target_pairs={{0,8},{8,0},{1,9},{9,1},{2,10},{10,2},{3,11},{11,3},{4,12},{12,4},... | collective-permute-start | bytes 2211848 | tf_op jit(solution)/shard_map/ppermute | solution.py:296
  36.9 11.1 %collective-permute-start.10 = (bf16[2,192,640]{2,1,0:T(8,128)(2,1)S(1)}, bf16[2,192,640]{2,1,0:T(8,128)(2,1)}, u32[]{:S(2)}, u32[]{:S(2)}) collective-permute-start(bf16[2,192,640]{2,1,0:T(8,128)(2,1)S(1)} %collective-permute-done.1.refs_1_.refs_4_), channel_id=1, source_target_pairs={{0,8},{8,0},{1,9},{9,1},{2,10},{10,2},{3,11},{11,3},{4,12},{12,4},... | collective-permute-start | bytes 1474568 | tf_op jit(solution)/shard_map/ppermute | solution.py:296
  37.0 11.0 %collective-permute-start.9 = (bf16[2,192,640]{2,1,0:T(8,128)(2,1)S(1)}, bf16[2,192,640]{2,1,0:T(8,128)(2,1)}, u32[]{:S(2)}, u32[]{:S(2)}) collective-permute-start(bf16[2,192,640]{2,1,0:T(8,128)(2,1)S(1)} %collective-permute-done.refs_0_.refs_2_), channel_id=1, source_target_pairs={{0,8},{8,0},{1,9},{9,1},{2,10},{10,2},{3,11},{11,3},{4,12},{12,4},... | collective-permute-start | bytes 1474568 | tf_op jit(solution)/shard_map/ppermute | solution.py:296
  37.4 10.6 %collective-permute-start.12 = (bf16[192,640]{1,0:T(8,128)(2,1)S(1)}, bf16[192,640]{1,0:T(8,128)(2,1)}, u32[]{:S(2)}, u32[]{:S(2)}) collective-permute-start(bf16[192,640]{1,0:T(8,128)(2,1)S(1)} %collective-permute-done.6.refs_5_.refs_8_), channel_id=1, source_target_pairs={{0,8},{8,0},{1,9},{9,1},{2,10},{10,2},{3,11},{11,3},{4,12},{12,4},... | collective-permute-start | bytes 737288 | tf_op jit(solution)/shard_map/ppermute | solution.py:296
  37.5 0.8 %copy-start = (bf16[2,192,640]{2,1,0:T(8,128)(2,1)}, bf16[2,192,640]{2,1,0:T(8,128)(2,1)S(1)}, u32[]{:S(2)}) copy-start(bf16[2,192,640]{2,1,0:T(8,128)(2,1)S(1)} %collective-permute-done.8.refs_1_) | copy-start | bytes 1474564
  38.3 9.7 %collective-permute-start.11 = (bf16[192,640]{1,0:T(8,128)(2,1)S(1)}, bf16[192,640]{1,0:T(8,128)(2,1)}, u32[]{:S(2)}, u32[]{:S(2)}) collective-permute-start(bf16[192,640]{1,0:T(8,128)(2,1)S(1)} %collective-permute-done.5.refs_4_.refs_6_), channel_id=1, source_target_pairs={{0,8},{8,0},{1,9},{9,1},{2,10},{10,2},{3,11},{11,3},{4,12},{12,4},... | collective-permute-start | bytes 737288 | tf_op jit(solution)/shard_map/ppermute | solution.py:296
  47.7 1.0 %copy-start.1 = (bf16[2,192,640]{2,1,0:T(8,128)(2,1)S(1)}, bf16[2,192,640]{2,1,0:T(8,128)(2,1)}, u32[]{:S(2)}) copy-start(bf16[2,192,640]{2,1,0:T(8,128)(2,1)} %copy-done) | copy-start | bytes 1474564

commit v3 on v2

--- a/solution.py
+++ b/solution.py
@@ -15,6 +15,8 @@
 
 FRAMES = ("zh", "y", "c")
 GROUPS = ("zl", "x")
+PLANE = ("zh", "x", "zl")
+NX, NZL = 4, 2
 NZ, NY, NC, NG = 4, 4, 2, 8
 HERE = HEADS // NG
 WIDE = HERE * HEAD_DIM
@@ -28,7 +30,9 @@
 CHUNKS = NZ * NG
 QROWS = CHUNKS * HOME
 SKEYS = NY * NG * HOME
+KEYS = NHIST + NC * SKEYS
 PIECES = 10
+HEAD_PARTS = ((0, 2), (2, 5))
 SCALE = math.log2(math.e) / math.sqrt(HEAD_DIM)
 F32, BF16 = jnp.float32, jnp.bfloat16
 
@@ -39,7 +43,12 @@
 
 IN_VMEM = pl.BlockSpec(memory_space=pltpu.VMEM)
 IN_SMEM = pl.BlockSpec(memory_space=pltpu.SMEM)
+IN_HBM = pl.BlockSpec(memory_space=pltpu.HBM)
 ANYWHERE = pl.BlockSpec(memory_space=pl.ANY)
+
+
+def group_of(m):
+    return (m % NZL) * NX + m // NZL
 
 
 def pack_kernel(x_ref, q_ref, kv_ref, q_rows, kv_rows):
@@ -54,8 +63,9 @@
             low += ROWS
             kv_rows[g, low : low + HOME, :] = x_ref[2, :, cols].astype(F32)
         q = q_rows[g].astype(BF16)
+        member = (g % NX) * NZL + g // NX
         for z in range(NZ):
-            q_ref[z * NG + g] = q
+            q_ref[z * NG + member] = q
         kv_ref[g] = kv_rows[g].astype(BF16)
 
 
@@ -105,7 +115,7 @@
         for e in range(HERE):
             for t in range(HOME):
                 row = (i * HERE + e) * HOME + t
-                o_ref[i, e, t * CHUNKS : (t + 1) * CHUNKS, :] = rows[
+                o_ref[i, t * CHUNKS : (t + 1) * CHUNKS, e * HEAD_DIM : (e + 1) * HEAD_DIM] = rows[
                     pl.ds(row, CHUNKS, stride=KV_CHUNK), :
                 ].astype(BF16)
 
@@ -113,7 +123,7 @@
 def sort_span(span, *after):
     return pl.pallas_call(
         sort_kernel,
-        out_shape=jax.ShapeDtypeStruct((2, HERE, SKEYS, HEAD_DIM), BF16),
+        out_shape=jax.ShapeDtypeStruct((2, SKEYS, WIDE), BF16),
         in_specs=[ANYWHERE] * (NY + len(after)),
         out_specs=IN_VMEM,
         scratch_shapes=[
@@ -126,59 +136,48 @@
     )(*span, *after)
 
 
-def sort_queries_kernel(x_ref, o_ref, rows):
-    rows[...] = x_ref[...].astype(F32).reshape(CHUNKS * CHUNK, HEAD_DIM)
-    for e in range(HERE):
-        for t in range(HOME):
-            row = e * HOME + t
-            o_ref[e, t * CHUNKS : (t + 1) * CHUNKS, :] = rows[
-                pl.ds(row, CHUNKS, stride=CHUNK), :
-            ].astype(BF16)
-
-
-def sort_queries(x):
-    return pl.pallas_call(
-        sort_queries_kernel,
-        out_shape=jax.ShapeDtypeStruct((HERE, QROWS, HEAD_DIM), BF16),
-        in_specs=[IN_VMEM],
-        out_specs=IN_VMEM,
-        scratch_shapes=[pltpu.VMEM((CHUNKS * CHUNK, HEAD_DIM), F32)],
-        compiler_params=params(8),
-    )(x)
-
-
-def keys_and_values(refs):
-    whole = [(refs[n].at[0], refs[n].at[1]) for n in range(6)]
-    return whole + [(refs[6], refs[8]), (refs[7], refs[9])]
-
-
 def against(queries, keys):
     return lax.dot_general(
         queries, keys, (((1,), (1,)), ((), ())), preferred_element_type=F32
     )
 
 
-def attend_kernel(place, q_ref, own_span, other_span, *refs):
-    hist = keys_and_values(refs[:PIECES])
-    o_ref, q_all, rows, kv_span, k_hist, v_hist, sums, tops, totals = refs[PIECES : PIECES + 9]
-    q_sem, span_sems, sems = refs[PIECES + 9 :]
+def attend_kernel(place, q_ref, *refs):
+    o_ref, kv_all, q_all, rows, sems = refs[PIECES + NC :]
+    k_ref, v_ref = kv_all.at[0], kv_all.at[1]
+    copies = []
+    for n, (low, high) in enumerate(HEAD_PARTS):
+        cols = pl.ds(low * HEAD_DIM, (high - low) * HEAD_DIM)
+        moves = []
+        for m in range(6):
+            moves.append((refs[m].at[:, :, cols], kv_all.at[:, pl.ds(m * HKEYS, HKEYS), cols]))
+        for m in range(2):
+            where = pl.ds((6 + m) * HKEYS, HKEYS)
+            moves.append((refs[6 + m].at[:, cols], k_ref.at[where, cols]))
+            moves.append((refs[8 + m].at[:, cols], v_ref.at[where, cols]))
+        for b in range(NC):
+            where = pl.ds(NHIST + b * SKEYS, SKEYS)
+            moves.append((refs[PIECES + b].at[:, :, cols], kv_all.at[:, where, cols]))
+        copies.append(
+            [pltpu.make_async_copy(x, to, sems.at[n, m]) for m, (x, to) in enumerate(moves)]
+        )
+        for copy in copies[n]:
+            copy.start()
+    rows[...] = q_ref[...].astype(F32).reshape(CHUNKS * CHUNK, HEAD_DIM)
+    for e in range(HERE):
+        for t in range(HOME):
+            row = e * HOME + t
+            q_all[e, t * CHUNKS : (t + 1) * CHUNKS, :] = rows[
+                pl.ds(row, CHUNKS, stride=CHUNK), :
+            ].astype(BF16)
+
     zh, y, c = place[0], place[1], place[2]
-    early, late = [], []
-    early.append(pltpu.make_async_copy(q_ref, q_all, q_sem.at[0]))
-    for b, source in enumerate((own_span, other_span)):
-        where = kv_span.at[:, :, pl.ds(b * SKEYS, SKEYS)]
-        early.append(pltpu.make_async_copy(source, where, span_sems.at[b]))
-    for n, (keys, values) in enumerate(hist):
-        where = pl.ds(n * HKEYS, HKEYS)
-        late.append(pltpu.make_async_copy(keys, k_hist.at[where], sems.at[0, n]))
-        late.append(pltpu.make_async_copy(values, v_hist.at[where], sems.at[1, n]))
-    for copy in early + late:
-        copy.start()
-
     row = lax.broadcasted_iota(jnp.int32, (QROWS, 1), 0)
     sender = lax.rem(row, CHUNKS)
     index = ((sender // NG) * NY + y) * NC + c
-    q_token = index * OWN + lax.rem(sender, NG) * HOME + row // CHUNKS
+    member = lax.rem(sender, NG)
+    group = lax.rem(member, NZL) * NX + member // NZL
+    q_token = index * OWN + group * HOME + row // CHUNKS
     q_frame = q_token // FRAME_LEN
     col = lax.broadcasted_iota(jnp.int32, (1, NC * SKEYS), 1)
     core = jnp.where(col < SKEYS, c, 1 - c)
@@ -186,34 +185,29 @@
     sender = lax.rem(col, CHUNKS)
     index = (zh * NY + lax.rem(y + NY - sender // NG, NY)) * NC + core
     k_token = index * OWN + lax.rem(sender, NG) * HOME + col // CHUNKS
-    allowed = q_frame >= k_token // FRAME_LEN
-
-    for copy in early:
-        copy.wait()
-    for e in range(HERE):
-        score = jnp.where(allowed, against(q_all[e], kv_span[0, e]), -1e30)
-        top = jnp.max(score, axis=1, keepdims=True)
-        weight = jnp.exp2((score - top) * SCALE)
-        tops[e] = jnp.broadcast_to(top, (QROWS, HEAD_DIM))
-        totals[e] = jnp.broadcast_to(
-            jnp.sum(weight, axis=1, keepdims=True), (QROWS, HEAD_DIM)
-        )
-        sums[e] = jnp.dot(weight.astype(BF16), kv_span[1, e], preferred_element_type=F32)
-    for copy in late:
-        copy.wait()
+    k_frame = k_token // FRAME_LEN
+
     lane = lax.broadcasted_iota(jnp.int32, (CHUNKS, HEAD_DIM), 1)
     lses = jnp.zeros((CHUNKS, HEAD_DIM), F32)
+    starts = {low: copies[n] for n, (low, high) in enumerate(HEAD_PARTS)}
+    upcoming = None
     for e in range(HERE):
-        cols = slice(e * HEAD_DIM, (e + 1) * HEAD_DIM)
-        score = against(q_all[e], k_hist[:, cols])
-        before = tops[e]
-        top = jnp.maximum(before, jnp.max(score, axis=1, keepdims=True))
-        factor = jnp.exp2((before - top) * SCALE)
-        weight = jnp.exp2((score - top[:, :1]) * SCALE)
-        total = totals[e] * factor + jnp.sum(weight, axis=1, keepdims=True)
-        summed = sums[e] * factor + jnp.dot(
-            weight.astype(BF16), v_hist[:, cols], preferred_element_type=F32
+        for copy in starts.get(e, []) if e == 0 else []:
+            copy.wait()
+        score = against(q_all[0], k_ref[:, :HEAD_DIM]) if e == 0 else upcoming
+        for copy in starts.get(e + 1, []):
+            copy.wait()
+        if e + 1 < HERE:
+            upcoming = against(q_all[e + 1], k_ref[:, (e + 1) * HEAD_DIM : (e + 2) * HEAD_DIM])
+        s_hist = score[:, :NHIST]
+        s_span = jnp.where(q_frame >= k_frame, score[:, NHIST:], -1e30)
+        top = jnp.maximum(
+            jnp.max(s_hist, axis=1, keepdims=True), jnp.max(s_span, axis=1, keepdims=True)
         )
+        weight = jnp.exp2((jnp.concatenate([s_hist, s_span], axis=1) - top) * SCALE)
+        total = jnp.sum(weight, axis=1, keepdims=True)
+        values = v_ref[:, e * HEAD_DIM : (e + 1) * HEAD_DIM]
+        summed = jnp.dot(weight.astype(BF16), values, preferred_element_type=F32)
         partial = summed / total
         lse = top * SCALE + jnp.log2(total)
         for t in range(HOME):
@@ -229,42 +223,34 @@
     o_ref[...] = rows[...].reshape(CHUNKS, CHUNK, HEAD_DIM).astype(BF16)
 
 
-def attend(place, q, own_span, other_span, hist):
-    keys = NHIST + NC * SKEYS
-    by_head = pltpu.VMEM((HERE, QROWS, HEAD_DIM), F32)
+def attend(place, q, hist, spans):
     return pl.pallas_call(
         attend_kernel,
         out_shape=jax.ShapeDtypeStruct((CHUNKS, CHUNK, HEAD_DIM), BF16),
-        in_specs=[IN_SMEM] + [ANYWHERE] * (3 + PIECES),
+        in_specs=[IN_SMEM, IN_VMEM] + [ANYWHERE] * (PIECES + NC),
         out_specs=IN_VMEM,
         scratch_shapes=[
+            pltpu.VMEM((2, KEYS, WIDE), BF16),
             pltpu.VMEM((HERE, QROWS, HEAD_DIM), BF16),
             pltpu.VMEM((CHUNKS * CHUNK, HEAD_DIM), F32),
-            pltpu.VMEM((2, HERE, NC * SKEYS, HEAD_DIM), BF16),
-            pltpu.VMEM((NHIST, WIDE), BF16),
-            pltpu.VMEM((NHIST, WIDE), BF16),
-            by_head,
-            by_head,
-            by_head,
-            pltpu.SemaphoreType.DMA((1,)),
-            pltpu.SemaphoreType.DMA((NC,)),
-            pltpu.SemaphoreType.DMA((2, NY * NC)),
+            pltpu.SemaphoreType.DMA((len(HEAD_PARTS), PIECES + NC)),
         ],
         compiler_params=params(24),
         cost_estimate=pl.CostEstimate(
-            flops=4 * QROWS * keys * WIDE,
-            bytes_accessed=4 * keys * WIDE,
-            transcendentals=QROWS * keys * HERE,
+            flops=4 * QROWS * KEYS * WIDE,
+            bytes_accessed=4 * KEYS * WIDE,
+            transcendentals=QROWS * KEYS * HERE,
         ),
-    )(place, q, own_span, other_span, *hist)
+    )(place, q, *hist, *spans)
 
 
 def merge_kernel(x_ref, o_ref, rows):
     eye = lax.broadcasted_iota(jnp.int32, (CHUNK, HEAD_DIM), 0) == lax.broadcasted_iota(
         jnp.int32, (CHUNK, HEAD_DIM), 1
     )
-    for g in range(NG):
-        parts = [x_ref[z * NG + g].astype(F32) for z in range(NZ)]
+    for m in range(NG):
+        g = group_of(m)
+        parts = [x_ref[z * NG + m].astype(F32) for z in range(NZ)]
         lses = [
             (p[ROWS : ROWS + 1] + p[ROWS + 1 : ROWS + 2]) + p[ROWS + 2 : ROWS + 3] for p in parts
         ]
@@ -312,10 +298,10 @@
 
     q, kv = pack(span_qkv)
     kv = after(exchange(kv, GROUPS), back, ahead)
-    q = exchange(q, ("zh",) + GROUPS)
+    q = exchange(q, PLANE)
     span = sort_span([kv] + [from_back(kv, "y", NY, d) for d in range(1, NY)], keys, values)
-    partial = attend(place, sort_queries(q), span, other(span), hist)
-    return merge(exchange(partial, ("zh",) + GROUPS))
+    partial = attend(place, q, hist, [span, other(span)])
+    return merge(exchange(partial, PLANE))
 
 
 def solution(mesh):

time: 78.3 us -> 73.9 us (0.944)
  Pallas kernels: 14.7 us -> 11.3 us
  starting transfers between devices: 28.7 us -> 26.6 us
  blocking collectives: 17.6 us -> 19.3 us
  waiting for transfers between devices: 13.9 us -> 12.6 us
    pallas_call x1, Pallas kernels: 10.5 us -> 7.3 us  [attend(): pl.pallas_call(attend_kernel, out_shape=jax.ShapeDtypeStruct((CHUNKS, CHU...]
    all_to_all x1, blocking collectives: 17.6 us -> 19.3 us  [exchange(): return lax.all_to_all(x, axes, split_axis=0, concat_axis=0, tiled=True)]
    all_to_all x2, starting transfers between devices: 16.7 us -> 15.5 us  [exchange(): return lax.all_to_all(x, axes, split_axis=0, concat_axis=0, tiled=True)]
    all_to_all x2, waiting for transfers between devices: 10.2 us -> 9.19 us  [exchange(): return lax.all_to_all(x, axes, split_axis=0, concat_axis=0, tiled=True)]
    ppermute x13, starting transfers between devices: 12 us -> 11 us  [from_back(): return lax.ppermute(x, axis, [(i, (i + back) % size) for i in range(size)])]
    pallas_call x2 -> x1, Pallas kernels: 2.21 us -> 2.01 us  [sort_span(): pl.pallas_call(sort_kernel, out_shape=jax.ShapeDtypeStruct((2, SKEYS, WID...]
  transfers between devices with their start and end apart: 15 -> 15, of which waited for: 4 -> 3; matrix products, arithmetic and copies ran while one was open for 2% -> 2% of each run, Pallas kernels for 4% -> 4%
where the time goes in v3:
time: 73.9 us; the launch traced here: 72.9 us
  starting transfers between devices  26.6 us (36%)
  blocking collectives  19.3 us (26%)
  waiting for transfers between devices  12.6 us (17%)
  Pallas kernels  11.3 us (15%)
  local copies, waits for them, and re-layouts  2.99 us (4%)
    all_to_all x1, blocking collectives, exchange(): return lax.all_to_all(x, axes, split_axis=0, concat_axis=0, tiled=True)  19.3 us
    all_to_all x2, starting transfers between devices, exchange(): return lax.all_to_all(x, axes, split_axis=0, concat_axis=0, tiled=True)  15.5 us
    ppermute x13, starting transfers between devices, from_back(): return lax.ppermute(x, axis, [(i, (i + back) % size) for i in range(size)])  11 us
    all_to_all x2, waiting for transfers between devices, exchange(): return lax.all_to_all(x, axes, split_axis=0, concat_axis=0, tiled=True)  9.19 us
    pallas_call x1, Pallas kernels, attend(): pl.pallas_call(attend_kernel, out_shape=jax.ShapeDtypeStruct((CHUNKS, CHU...  7.3 us
    ppermute x13, waiting for transfers between devices, from_back(): return lax.ppermute(x, axis, [(i, (i + back) % size) for i in range(size)])  3.43 us
    unnamed x5, local copies, waits for them, and re-layouts  2.95 us
    pallas_call x1, Pallas kernels, sort_span(): pl.pallas_call(sort_kernel, out_shape=jax.ShapeDtypeStruct((2, SKEYS, WID...  2.01 us
  transfers between devices with their start and end apart: 15, of which 3 were waited for; matrix products, arithmetic and copies ran while one was open for 2% of the time, Pallas kernels for 4%

profile of v3, /device:TPU:8, one launch (start us, length us, event | category | flops | bytes accessed | tf_op | source)
XLA Modules:
  0.0 72.9 jit_solution(17800599479951500436)
XLA Ops:
  0.0 1.6 %collective-permute-start.1 = (bf16[2,192,640]{2,1,0:T(8,128)(2,1)}, bf16[2,192,640]{2,1,0:T(8,128)(2,1)S(1)}, u32[]{:S(2)}, u32[]{:S(2)}) collective-permute-start(bf16[2,192,640]{2,1,0:T(8,128)(2,1)} %refs_0_.1), channel_id=1, source_target_pairs={{0,16},{16,32},{32,48},{48,0},{1,17},{17,33},{33,49},{49,1},{2,18}... | collective-permute-start | bytes 1474568 | tf_op jit(solution)/shard_map/ppermute | solution.py:282
  1.6 0.6 collective-permute-start.3
  2.2 1.1 %copy.3.x_ref = bf16[3,9,5120]{2,1,0:T(8,128)(2,1)S(1)} copy(bf16[3,9,5120]{2,0,1:T(4,128)(2,1)} %param.2) | data formatting | bytes 552960 | tf_op args[0]
  3.3 1.0 %shard_map.28 = (bf16[32,48,128]{2,1,0:T(8,128)(2,1)}, bf16[8,96,128]{2,1,0:T(8,128)(2,1)}) custom-call(bf16[3,9,5120]{2,1,0:T(8,128)(2,1)S(1)} %copy.3.x_ref), custom_call_target="tpu_custom_call" | custom-call | tf_op jit(solution)/shard_map/pallas_call | solution.py:73
  4.3 5.5 %all-to-all-start.1 = ((bf16[8,96,128]{2,1,0:T(8,128)(2,1)}), bf16[8,96,128]{2,1,0:T(8,128)(2,1)S(1)}, u32[]{:S(2)}, u32[]{:S(2)}) async-start(bf16[8,96,128]{2,1,0:T(8,128)(2,1)} %get-tuple-element.8), calls=%async_computation.1 | async-start | bytes 393216 | tf_op jit(solution)/shard_map/all_to_all | solution.py:286
  9.8 3.4 %collective-permute-done.1.refs_0_.refs_2_ = bf16[2,192,640]{2,1,0:T(8,128)(2,1)S(1)} collective-permute-done((bf16[2,192,640]{2,1,0:T(8,128)(2,1)}, bf16[2,192,640]{2,1,0:T(8,128)(2,1)S(1)}, u32[]{:S(2)}, u32[]{:S(2)}) %collective-permute-start.1) | collective-permute-done | bytes 491552 | tf_op jit(solution)/shard_map/ppermute | solution.py:282
  13.2 1.7 %collective-permute-start.5 = (bf16[192,640]{1,0:T(8,128)(2,1)S(1)}, bf16[192,640]{1,0:T(8,128)(2,1)S(1)}, u32[]{:S(2)}, u32[]{:S(2)}) collective-permute-start(bf16[192,640]{1,0:T(8,128)(2,1)S(1)} %slice_bitcast_fusion.1), channel_id=1, source_target_pairs={{0,16},{16,32},{32,48},{48,0},{1,17},{17,33},{33,49},{49,1},{2,18}... | collective-permute-start | bytes 737288 | tf_op jit(solution)/shard_map/ppermute | solution.py:282
  14.9 0.5 collective-permute-start.7
  15.4 1.3 %all-to-all-done.1.x_ref = bf16[8,96,128]{2,1,0:T(8,128)(2,1)S(1)} async-done(((bf16[8,96,128]{2,1,0:T(8,128)(2,1)}), bf16[8,96,128]{2,1,0:T(8,128)(2,1)S(1)}, u32[]{:S(2)}, u32[]{:S(2)}) %all-to-all-start.1) | async-done | bytes 196640 | tf_op jit(solution)/shard_map/all_to_all | solution.py:286
  16.7 1.7 %collective-permute-start.11 = (bf16[8,96,128]{2,1,0:T(8,128)(2,1)S(1)}, bf16[8,96,128]{2,1,0:T(8,128)(2,1)S(1)}, u32[]{:S(2)}, u32[]{:S(2)}) collective-permute-start(bf16[8,96,128]{2,1,0:T(8,128)(2,1)S(1)} %shard_map.29.refs_0_), channel_id=1, source_target_pairs={{0,48},{16,0},{32,16},{48,32},{1,49},{17,1},{33,17},{49,33},{2,50}... | collective-permute-start | bytes 589832 | tf_op jit(solution)/shard_map/ppermute | solution.py:282
  18.5 1.4 %collective-permute-start.10 = (bf16[8,96,128]{2,1,0:T(8,128)(2,1)S(1)}, bf16[8,96,128]{2,1,0:T(8,128)(2,1)S(1)}, u32[]{:S(2)}, u32[]{:S(2)}) collective-permute-start(bf16[8,96,128]{2,1,0:T(8,128)(2,1)S(1)} %shard_map.29.refs_0_), channel_id=1, source_target_pairs={{0,32},{16,48},{32,0},{48,16},{1,33},{17,49},{33,1},{49,17},{2,34}... | collective-permute-start | bytes 589832 | tf_op jit(solution)/shard_map/ppermute | solution.py:282
  19.8 1.9 %collective-permute-start.9 = (bf16[8,96,128]{2,1,0:T(8,128)(2,1)S(1)}, bf16[8,96,128]{2,1,0:T(8,128)(2,1)S(1)}, u32[]{:S(2)}, u32[]{:S(2)}) collective-permute-start(bf16[8,96,128]{2,1,0:T(8,128)(2,1)S(1)} %shard_map.29.refs_0_), channel_id=1, source_target_pairs={{0,16},{16,32},{32,48},{48,0},{1,17},{17,33},{33,49},{49,1},{2,18}... | collective-permute-start | bytes 589832 | tf_op jit(solution)/shard_map/ppermute | solution.py:282
  21.7 10.0 %all-to-all-start = ((bf16[32,48,128]{2,1,0:T(8,128)(2,1)}), bf16[32,48,128]{2,1,0:T(8,128)(2,1)S(1)}, u32[]{:S(2)}, u32[]{:S(2)}) async-start(bf16[32,48,128]{2,1,0:T(8,128)(2,1)} %get-tuple-element.7), calls=%async_computation | async-start | bytes 786432 | tf_op jit(solution)/shard_map/all_to_all | solution.py:286
  31.9 2.0 %shard_map.30.refs_10_ = bf16[2,288,640]{2,1,0:T(8,128)(2,1)S(1)} custom-call(bf16[8,96,128]{2,1,0:T(8,128)(2,1)S(1)} %shard_map.29.refs_0_, bf16[8,96,128]{2,1,0:T(8,128)(2,1)S(1)} %collective-permute-done.9.refs_1_, bf16[8,96,128]{2,1,0:T(8,128)(2,1)S(1)} %collective-permute-done.10.refs_2_, bf16[8,96,128]{2,1,0:T(8,128)(2,1)S(1)} %collective-permute-done.11.refs_3_, ...), custom_call_target="tpu_custom_call" | custom-call | tf_op jit(solution)/shard_map/pallas_call | solution.py:124
  33.9 0.6 collective-permute-start.12
  34.5 0.1 collective-permute-start.2
  34.6 0.4 collective-permute-start.4
  35.1 0.8 %copy-done = bf16[2,192,640]{2,1,0:T(8,128)(2,1)} copy-done((bf16[2,192,640]{2,1,0:T(8,128)(2,1)}, bf16[2,192,640]{2,1,0:T(8,128)(2,1)S(1)}, u32[]{:S(2)}) %copy-start) | copy-done | bytes 491544
  35.9 0.4 collective-permute-start.8
  36.4 7.9 %all-to-all-done.q_ref = bf16[32,48,128]{2,1,0:T(8,128)(2,1)S(1)} async-done(((bf16[32,48,128]{2,1,0:T(8,128)(2,1)}), bf16[32,48,128]{2,1,0:T(8,128)(2,1)S(1)}, u32[]{:S(2)}, u32[]{:S(2)}) %all-to-all-start) | async-done | bytes 393248 | tf_op jit(solution)/shard_map/all_to_all | solution.py:286
  44.3 1.0 %copy-done.1 = bf16[2,192,640]{2,1,0:T(8,128)(2,1)S(1)} copy-done((bf16[2,192,640]{2,1,0:T(8,128)(2,1)S(1)}, bf16[2,192,640]{2,1,0:T(8,128)(2,1)}, u32[]{:S(2)}) %copy-start.1) | copy-done | bytes 491544
  45.4 7.3 %shard_map.31 = bf16[32,48,128]{2,1,0:T(8,128)(2,1)S(1)} custom-call(s32[3]{0:T(128)S(1)} %pad_add_fusion.place, bf16[32,48,128]{2,1,0:T(8,128)(2,1)S(1)} %all-to-all-done.q_ref, bf16[2,192,640]{2,1,0:T(8,128)(2,1)} %refs_0_.1, bf16[2,192,640]{2,1,0:T(8,128)(2,1)S(1)} %copy-done.1, bf16[2,192,640]{2,1,0:T(8,128)(2,1)S(1)} %collective-permute-done.1.refs_0_.refs_2_, ...), custom_call_target="tpu_custom_call" | custom-call | flops 1557135360 | bytes 5406720 | tf_op jit(solution)/shard_map/pallas_call | solution.py:227
  52.7 19.3 %all_to_all.15.x_ref = bf16[32,48,128]{2,1,0:T(8,128)(2,1)S(1)} all-to-all(bf16[32,48,128]{2,1,0:T(8,128)(2,1)S(1)} %shard_map.31), channel_id=1, replica_groups=mesh['zh'=4,'y'=4,'c'=2,'zl'=2,'x'=4] {'zh','x','zl'}, dimensions={0} | all-to-all | bytes 786432 | tf_op jit(solution)/shard_map/all_to_all | solution.py:286
  71.9 1.0 %shard_map.32 = bf16[9,5120]{1,0:T(8,128)(2,1)} custom-call(bf16[32,48,128]{2,1,0:T(8,128)(2,1)S(1)} %all_to_all.15.x_ref), custom_call_target="tpu_custom_call" | custom-call | tf_op jit(solution)/shard_map/pallas_call | solution.py:271
  (20 shorter events, 0.4 us)
Async XLA Ops:
  0.0 13.2 %collective-permute-start.1 = (bf16[2,192,640]{2,1,0:T(8,128)(2,1)}, bf16[2,192,640]{2,1,0:T(8,128)(2,1)S(1)}, u32[]{:S(2)}, u32[]{:S(2)}) collective-permute-start(bf16[2,192,640]{2,1,0:T(8,128)(2,1)} %refs_0_.1), channel_id=1, source_target_pairs={{0,16},{16,32},{32,48},{48,0},{1,17},{17,33},{33,49},{49,1},{2,18}... | collective-permute-start | bytes 1474568 | tf_op jit(solution)/shard_map/ppermute | solution.py:282
  1.6 13.3 %collective-permute-start.3 = (bf16[2,192,640]{2,1,0:T(8,128)(2,1)}, bf16[2,192,640]{2,1,0:T(8,128)(2,1)S(1)}, u32[]{:S(2)}, u32[]{:S(2)}) collective-permute-start(bf16[2,192,640]{2,1,0:T(8,128)(2,1)} %refs_0_.1), channel_id=1, source_target_pairs={{0,48},{16,0},{32,16},{48,32},{1,49},{17,1},{33,17},{49,33},{2,50}... | collective-permute-start | bytes 1474568 | tf_op jit(solution)/shard_map/ppermute | solution.py:282
  4.3 12.4 %all-to-all-start.1 = ((bf16[8,96,128]{2,1,0:T(8,128)(2,1)}), bf16[8,96,128]{2,1,0:T(8,128)(2,1)S(1)}, u32[]{:S(2)}, u32[]{:S(2)}) async-start(bf16[8,96,128]{2,1,0:T(8,128)(2,1)} %get-tuple-element.8), calls=%async_computation.1 | async-start | bytes 393216 | tf_op jit(solution)/shard_map/all_to_all | solution.py:286
  13.2 18.7 %collective-permute-start.5 = (bf16[192,640]{1,0:T(8,128)(2,1)S(1)}, bf16[192,640]{1,0:T(8,128)(2,1)S(1)}, u32[]{:S(2)}, u32[]{:S(2)}) collective-permute-start(bf16[192,640]{1,0:T(8,128)(2,1)S(1)} %slice_bitcast_fusion.1), channel_id=1, source_target_pairs={{0,16},{16,32},{32,48},{48,0},{1,17},{17,33},{33,49},{49,1},{2,18}... | collective-permute-start | bytes 737288 | tf_op jit(solution)/shard_map/ppermute | solution.py:282
  14.9 17.0 %collective-permute-start.7 = (bf16[192,640]{1,0:T(8,128)(2,1)S(1)}, bf16[192,640]{1,0:T(8,128)(2,1)S(1)}, u32[]{:S(2)}, u32[]{:S(2)}) collective-permute-start(bf16[192,640]{1,0:T(8,128)(2,1)S(1)} %slice_bitcast_fusion), channel_id=1, source_target_pairs={{0,48},{16,0},{32,16},{48,32},{1,49},{17,1},{33,17},{49,33},{2,50}... | collective-permute-start | bytes 737288 | tf_op jit(solution)/shard_map/ppermute | solution.py:282
  16.7 15.0 %collective-permute-start.11 = (bf16[8,96,128]{2,1,0:T(8,128)(2,1)S(1)}, bf16[8,96,128]{2,1,0:T(8,128)(2,1)S(1)}, u32[]{:S(2)}, u32[]{:S(2)}) collective-permute-start(bf16[8,96,128]{2,1,0:T(8,128)(2,1)S(1)} %shard_map.29.refs_0_), channel_id=1, source_target_pairs={{0,48},{16,0},{32,16},{48,32},{1,49},{17,1},{33,17},{49,33},{2,50}... | collective-permute-start | bytes 589832 | tf_op jit(solution)/shard_map/ppermute | solution.py:282
  18.5 13.4 %collective-permute-start.10 = (bf16[8,96,128]{2,1,0:T(8,128)(2,1)S(1)}, bf16[8,96,128]{2,1,0:T(8,128)(2,1)S(1)}, u32[]{:S(2)}, u32[]{:S(2)}) collective-permute-start(bf16[8,96,128]{2,1,0:T(8,128)(2,1)S(1)} %shard_map.29.refs_0_), channel_id=1, source_target_pairs={{0,32},{16,48},{32,0},{48,16},{1,33},{17,49},{33,1},{49,17},{2,34}... | collective-permute-start | bytes 589832 | tf_op jit(solution)/shard_map/ppermute | solution.py:282
  19.8 12.0 %collective-permute-start.9 = (bf16[8,96,128]{2,1,0:T(8,128)(2,1)S(1)}, bf16[8,96,128]{2,1,0:T(8,128)(2,1)S(1)}, u32[]{:S(2)}, u32[]{:S(2)}) collective-permute-start(bf16[8,96,128]{2,1,0:T(8,128)(2,1)S(1)} %shard_map.29.refs_0_), channel_id=1, source_target_pairs={{0,16},{16,32},{32,48},{48,0},{1,17},{17,33},{33,49},{49,1},{2,18}... | collective-permute-start | bytes 589832 | tf_op jit(solution)/shard_map/ppermute | solution.py:282
  21.7 22.6 %all-to-all-start = ((bf16[32,48,128]{2,1,0:T(8,128)(2,1)}), bf16[32,48,128]{2,1,0:T(8,128)(2,1)S(1)}, u32[]{:S(2)}, u32[]{:S(2)}) async-start(bf16[32,48,128]{2,1,0:T(8,128)(2,1)} %get-tuple-element.7), calls=%async_computation | async-start | bytes 786432 | tf_op jit(solution)/shard_map/all_to_all | solution.py:286
  31.8 3.3 %collective-permute-start = (bf16[2,192,640]{2,1,0:T(8,128)(2,1)}, bf16[2,192,640]{2,1,0:T(8,128)(2,1)S(1)}, u32[]{:S(2)}, u32[]{:S(2)}) collective-permute-start(bf16[2,192,640]{2,1,0:T(8,128)(2,1)} %refs_0_.1), channel_id=1, source_target_pairs={{0,8},{8,0},{1,9},{9,1},{2,10},{10,2},{3,11},{11,3},{4,12},{12,4},... | collective-permute-start | bytes 1474568 | tf_op jit(solution)/shard_map/ppermute | solution.py:282
  33.9 10.4 %collective-permute-start.12 = (bf16[2,288,640]{2,1,0:T(8,128)(2,1)S(1)}, bf16[2,288,640]{2,1,0:T(8,128)(2,1)S(1)}, u32[]{:S(2)}, u32[]{:S(2)}) collective-permute-start(bf16[2,288,640]{2,1,0:T(8,128)(2,1)S(1)} %shard_map.30.refs_10_), channel_id=1, source_target_pairs={{0,8},{8,0},{1,9},{9,1},{2,10},{10,2},{3,11},{11,3},{4,12},{12,4},... | collective-permute-start | bytes 2211848 | tf_op jit(solution)/shard_map/ppermute | solution.py:282
  34.5 9.8 %collective-permute-start.2 = (bf16[2,192,640]{2,1,0:T(8,128)(2,1)S(1)}, bf16[2,192,640]{2,1,0:T(8,128)(2,1)}, u32[]{:S(2)}, u32[]{:S(2)}) collective-permute-start(bf16[2,192,640]{2,1,0:T(8,128)(2,1)S(1)} %collective-permute-done.1.refs_0_.refs_2_), channel_id=1, source_target_pairs={{0,8},{8,0},{1,9},{9,1},{2,10},{10,2},{3,11},{11,3},{4,12},{12,4},... | collective-permute-start | bytes 1474568 | tf_op jit(solution)/shard_map/ppermute | solution.py:282
  34.6 9.7 %collective-permute-start.4 = (bf16[2,192,640]{2,1,0:T(8,128)(2,1)S(1)}, bf16[2,192,640]{2,1,0:T(8,128)(2,1)}, u32[]{:S(2)}, u32[]{:S(2)}) collective-permute-start(bf16[2,192,640]{2,1,0:T(8,128)(2,1)S(1)} %collective-permute-done.3.refs_1_.refs_4_), channel_id=1, source_target_pairs={{0,8},{8,0},{1,9},{9,1},{2,10},{10,2},{3,11},{11,3},{4,12},{12,4},... | collective-permute-start | bytes 1474568 | tf_op jit(solution)/shard_map/ppermute | solution.py:282
  35.0 9.3 %collective-permute-start.6 = (bf16[192,640]{1,0:T(8,128)(2,1)S(1)}, bf16[192,640]{1,0:T(8,128)(2,1)}, u32[]{:S(2)}, u32[]{:S(2)}) collective-permute-start(bf16[192,640]{1,0:T(8,128)(2,1)S(1)} %collective-permute-done.5.refs_4_.refs_6_), channel_id=1, source_target_pairs={{0,8},{8,0},{1,9},{9,1},{2,10},{10,2},{3,11},{11,3},{4,12},{12,4},... | collective-permute-start | bytes 737288 | tf_op jit(solution)/shard_map/ppermute | solution.py:282
  35.1 0.8 %copy-start = (bf16[2,192,640]{2,1,0:T(8,128)(2,1)}, bf16[2,192,640]{2,1,0:T(8,128)(2,1)S(1)}, u32[]{:S(2)}) copy-start(bf16[2,192,640]{2,1,0:T(8,128)(2,1)S(1)} %collective-permute-done.refs_1_) | copy-start | bytes 1474564
  35.9 8.4 %collective-permute-start.8 = (bf16[192,640]{1,0:T(8,128)(2,1)S(1)}, bf16[192,640]{1,0:T(8,128)(2,1)}, u32[]{:S(2)}, u32[]{:S(2)}) collective-permute-start(bf16[192,640]{1,0:T(8,128)(2,1)S(1)} %collective-permute-done.7.refs_5_.refs_8_), channel_id=1, source_target_pairs={{0,8},{8,0},{1,9},{9,1},{2,10},{10,2},{3,11},{11,3},{4,12},{12,4},... | collective-permute-start | bytes 737288 | tf_op jit(solution)/shard_map/ppermute | solution.py:282
  44.3 1.0 %copy-start.1 = (bf16[2,192,640]{2,1,0:T(8,128)(2,1)S(1)}, bf16[2,192,640]{2,1,0:T(8,128)(2,1)}, u32[]{:S(2)}) copy-start(bf16[2,192,640]{2,1,0:T(8,128)(2,1)} %copy-done) | copy-start | bytes 1474564

commit v4 on v3

--- a/solution.py
+++ b/solution.py
@@ -79,8 +79,8 @@
         in_specs=[IN_VMEM],
         out_specs=(IN_VMEM, IN_VMEM),
         scratch_shapes=[
-            pltpu.VMEM((NG, CHUNK, HEAD_DIM), F32),
-            pltpu.VMEM((NG, KV_CHUNK, HEAD_DIM), F32),
+            pltpu.VMEM((NG + 1, CHUNK, HEAD_DIM), F32),
+            pltpu.VMEM((NG + 1, KV_CHUNK, HEAD_DIM), F32),
         ],
         compiler_params=params(8),
     )(x)
@@ -110,7 +110,9 @@
         copy.start()
     for copy in copies:
         copy.wait()
-    rows[...] = chunks[...].astype(F32).reshape(CHUNKS * KV_CHUNK, HEAD_DIM)
+    rows[: CHUNKS * KV_CHUNK, :] = (
+        chunks[...].astype(F32).reshape(CHUNKS * KV_CHUNK, HEAD_DIM)
+    )
     for i in range(2):
         for e in range(HERE):
             for t in range(HOME):
@@ -128,7 +130,7 @@
         out_specs=IN_VMEM,
         scratch_shapes=[
             pltpu.VMEM((CHUNKS, KV_CHUNK, HEAD_DIM), BF16),
-            pltpu.VMEM((CHUNKS * KV_CHUNK, HEAD_DIM), F32),
+            pltpu.VMEM(((CHUNKS + 1) * KV_CHUNK, HEAD_DIM), F32),
             pltpu.SemaphoreType.DMA((NY,)),
         ],
         compiler_params=params(8),
@@ -163,7 +165,7 @@
         )
         for copy in copies[n]:
             copy.start()
-    rows[...] = q_ref[...].astype(F32).reshape(CHUNKS * CHUNK, HEAD_DIM)
+    rows[: CHUNKS * CHUNK, :] = q_ref[...].astype(F32).reshape(CHUNKS * CHUNK, HEAD_DIM)
     for e in range(HERE):
         for t in range(HOME):
             row = e * HOME + t
@@ -220,7 +222,8 @@
     middle = (lses - high).astype(BF16).astype(F32)
     for n, term in enumerate((high, middle, lses - high - middle)):
         rows[pl.ds(ROWS + n, CHUNKS, stride=CHUNK), :] = term
-    o_ref[...] = rows[...].reshape(CHUNKS, CHUNK, HEAD_DIM).astype(BF16)
+    chunks = rows[: CHUNKS * CHUNK, :].reshape(CHUNKS, CHUNK, HEAD_DIM)
+    o_ref[...] = chunks.astype(BF16)
 
 
 def attend(place, q, hist, spans):
@@ -232,7 +235,7 @@
         scratch_shapes=[
             pltpu.VMEM((2, KEYS, WIDE), BF16),
             pltpu.VMEM((HERE, QROWS, HEAD_DIM), BF16),
-            pltpu.VMEM((CHUNKS * CHUNK, HEAD_DIM), F32),
+            pltpu.VMEM(((CHUNKS + 1) * CHUNK, HEAD_DIM), F32),
             pltpu.SemaphoreType.DMA((len(HEAD_PARTS), PIECES + NC)),
         ],
         compiler_params=params(24),
@@ -273,7 +276,7 @@
         out_shape=jax.ShapeDtypeStruct((HOME, HEADS * HEAD_DIM), BF16),
         in_specs=[IN_VMEM],
         out_specs=IN_VMEM,
-        scratch_shapes=[pltpu.VMEM((NG, CHUNK, HEAD_DIM), F32)],
+        scratch_shapes=[pltpu.VMEM((NG + 1, CHUNK, HEAD_DIM), F32)],
         compiler_params=params(8),
     )(x)
 

time: 73.9 us -> 73.9 us (level)
  no operation moved by 1% of the time
where the time goes in v4:
time: 73.9 us; the launch traced here: 72.9 us
  starting transfers between devices  26.6 us (36%)
  blocking collectives  19.3 us (26%)
  waiting for transfers between devices  12.6 us (17%)
  Pallas kernels  11.3 us (15%)
  local copies, waits for them, and re-layouts  2.99 us (4%)
    all_to_all x1, blocking collectives, exchange(): return lax.all_to_all(x, axes, split_axis=0, concat_axis=0, tiled=True)  19.3 us
    all_to_all x2, starting transfers between devices, exchange(): return lax.all_to_all(x, axes, split_axis=0, concat_axis=0, tiled=True)  15.5 us
    ppermute x13, starting transfers between devices, from_back(): return lax.ppermute(x, axis, [(i, (i + back) % size) for i in range(size)])  11 us
    all_to_all x2, waiting for transfers between devices, exchange(): return lax.all_to_all(x, axes, split_axis=0, concat_axis=0, tiled=True)  9.19 us
    pallas_call x1, Pallas kernels, attend(): pl.pallas_call(attend_kernel, out_shape=jax.ShapeDtypeStruct((CHUNKS, CHU...  7.29 us
    ppermute x13, waiting for transfers between devices, from_back(): return lax.ppermute(x, axis, [(i, (i + back) % size) for i in range(size)])  3.43 us
    unnamed x5, local copies, waits for them, and re-layouts  2.95 us
    pallas_call x1, Pallas kernels, sort_span(): pl.pallas_call(sort_kernel, out_shape=jax.ShapeDtypeStruct((2, SKEYS, WID...  2.01 us
  transfers between devices with their start and end apart: 15, of which 3 were waited for; matrix products, arithmetic and copies ran while one was open for 2% of the time, Pallas kernels for 4%

profile of v4, /device:TPU:8, one launch (start us, length us, event | category | flops | bytes accessed | tf_op | source)
XLA Modules:
  0.0 72.9 jit_solution(15138964488351096650)
XLA Ops:
  0.0 1.6 %collective-permute-start.1 = (bf16[2,192,640]{2,1,0:T(8,128)(2,1)}, bf16[2,192,640]{2,1,0:T(8,128)(2,1)S(1)}, u32[]{:S(2)}, u32[]{:S(2)}) collective-permute-start(bf16[2,192,640]{2,1,0:T(8,128)(2,1)} %refs_0_.1), channel_id=1, source_target_pairs={{0,16},{16,32},{32,48},{48,0},{1,17},{17,33},{33,49},{49,1},{2,18}... | collective-permute-start | bytes 1474568 | tf_op jit(solution)/shard_map/ppermute | solution.py:285
  1.6 0.6 collective-permute-start.3
  2.2 1.1 %copy.3.x_ref = bf16[3,9,5120]{2,1,0:T(8,128)(2,1)S(1)} copy(bf16[3,9,5120]{2,0,1:T(4,128)(2,1)} %param.2) | data formatting | bytes 552960 | tf_op args[0]
  3.3 1.0 %shard_map.28 = (bf16[32,48,128]{2,1,0:T(8,128)(2,1)}, bf16[8,96,128]{2,1,0:T(8,128)(2,1)}) custom-call(bf16[3,9,5120]{2,1,0:T(8,128)(2,1)S(1)} %copy.3.x_ref), custom_call_target="tpu_custom_call" | custom-call | tf_op jit(solution)/shard_map/pallas_call | solution.py:73
  4.3 5.5 %all-to-all-start.1 = ((bf16[8,96,128]{2,1,0:T(8,128)(2,1)}), bf16[8,96,128]{2,1,0:T(8,128)(2,1)S(1)}, u32[]{:S(2)}, u32[]{:S(2)}) async-start(bf16[8,96,128]{2,1,0:T(8,128)(2,1)} %get-tuple-element.8), calls=%async_computation.1 | async-start | bytes 393216 | tf_op jit(solution)/shard_map/all_to_all | solution.py:289
  9.8 3.4 %collective-permute-done.1.refs_0_.refs_2_ = bf16[2,192,640]{2,1,0:T(8,128)(2,1)S(1)} collective-permute-done((bf16[2,192,640]{2,1,0:T(8,128)(2,1)}, bf16[2,192,640]{2,1,0:T(8,128)(2,1)S(1)}, u32[]{:S(2)}, u32[]{:S(2)}) %collective-permute-start.1) | collective-permute-done | bytes 491552 | tf_op jit(solution)/shard_map/ppermute | solution.py:285
  13.2 1.7 %collective-permute-start.5 = (bf16[192,640]{1,0:T(8,128)(2,1)S(1)}, bf16[192,640]{1,0:T(8,128)(2,1)S(1)}, u32[]{:S(2)}, u32[]{:S(2)}) collective-permute-start(bf16[192,640]{1,0:T(8,128)(2,1)S(1)} %slice_bitcast_fusion.1), channel_id=1, source_target_pairs={{0,16},{16,32},{32,48},{48,0},{1,17},{17,33},{33,49},{49,1},{2,18}... | collective-permute-start | bytes 737288 | tf_op jit(solution)/shard_map/ppermute | solution.py:285
  14.9 0.5 collective-permute-start.7
  15.4 1.3 %all-to-all-done.1.x_ref = bf16[8,96,128]{2,1,0:T(8,128)(2,1)S(1)} async-done(((bf16[8,96,128]{2,1,0:T(8,128)(2,1)}), bf16[8,96,128]{2,1,0:T(8,128)(2,1)S(1)}, u32[]{:S(2)}, u32[]{:S(2)}) %all-to-all-start.1) | async-done | bytes 196640 | tf_op jit(solution)/shard_map/all_to_all | solution.py:289
  16.7 1.7 %collective-permute-start.11 = (bf16[8,96,128]{2,1,0:T(8,128)(2,1)S(1)}, bf16[8,96,128]{2,1,0:T(8,128)(2,1)S(1)}, u32[]{:S(2)}, u32[]{:S(2)}) collective-permute-start(bf16[8,96,128]{2,1,0:T(8,128)(2,1)S(1)} %shard_map.29.refs_0_), channel_id=1, source_target_pairs={{0,48},{16,0},{32,16},{48,32},{1,49},{17,1},{33,17},{49,33},{2,50}... | collective-permute-start | bytes 589832 | tf_op jit(solution)/shard_map/ppermute | solution.py:285
  18.5 1.4 %collective-permute-start.10 = (bf16[8,96,128]{2,1,0:T(8,128)(2,1)S(1)}, bf16[8,96,128]{2,1,0:T(8,128)(2,1)S(1)}, u32[]{:S(2)}, u32[]{:S(2)}) collective-permute-start(bf16[8,96,128]{2,1,0:T(8,128)(2,1)S(1)} %shard_map.29.refs_0_), channel_id=1, source_target_pairs={{0,32},{16,48},{32,0},{48,16},{1,33},{17,49},{33,1},{49,17},{2,34}... | collective-permute-start | bytes 589832 | tf_op jit(solution)/shard_map/ppermute | solution.py:285
  19.8 1.9 %collective-permute-start.9 = (bf16[8,96,128]{2,1,0:T(8,128)(2,1)S(1)}, bf16[8,96,128]{2,1,0:T(8,128)(2,1)S(1)}, u32[]{:S(2)}, u32[]{:S(2)}) collective-permute-start(bf16[8,96,128]{2,1,0:T(8,128)(2,1)S(1)} %shard_map.29.refs_0_), channel_id=1, source_target_pairs={{0,16},{16,32},{32,48},{48,0},{1,17},{17,33},{33,49},{49,1},{2,18}... | collective-permute-start | bytes 589832 | tf_op jit(solution)/shard_map/ppermute | solution.py:285
  21.7 10.0 %all-to-all-start = ((bf16[32,48,128]{2,1,0:T(8,128)(2,1)}), bf16[32,48,128]{2,1,0:T(8,128)(2,1)S(1)}, u32[]{:S(2)}, u32[]{:S(2)}) async-start(bf16[32,48,128]{2,1,0:T(8,128)(2,1)} %get-tuple-element.7), calls=%async_computation | async-start | bytes 786432 | tf_op jit(solution)/shard_map/all_to_all | solution.py:289
  31.9 2.0 %shard_map.30.refs_10_ = bf16[2,288,640]{2,1,0:T(8,128)(2,1)S(1)} custom-call(bf16[8,96,128]{2,1,0:T(8,128)(2,1)S(1)} %shard_map.29.refs_0_, bf16[8,96,128]{2,1,0:T(8,128)(2,1)S(1)} %collective-permute-done.9.refs_1_, bf16[8,96,128]{2,1,0:T(8,128)(2,1)S(1)} %collective-permute-done.10.refs_2_, bf16[8,96,128]{2,1,0:T(8,128)(2,1)S(1)} %collective-permute-done.11.refs_3_, ...), custom_call_target="tpu_custom_call" | custom-call | tf_op jit(solution)/shard_map/pallas_call | solution.py:126
  33.9 0.6 collective-permute-start.12
  34.5 0.1 collective-permute-start.2
  34.6 0.4 collective-permute-start.4
  35.1 0.8 %copy-done = bf16[2,192,640]{2,1,0:T(8,128)(2,1)} copy-done((bf16[2,192,640]{2,1,0:T(8,128)(2,1)}, bf16[2,192,640]{2,1,0:T(8,128)(2,1)S(1)}, u32[]{:S(2)}) %copy-start) | copy-done | bytes 491544
  35.9 0.4 collective-permute-start.8
  36.4 7.9 %all-to-all-done.q_ref = bf16[32,48,128]{2,1,0:T(8,128)(2,1)S(1)} async-done(((bf16[32,48,128]{2,1,0:T(8,128)(2,1)}), bf16[32,48,128]{2,1,0:T(8,128)(2,1)S(1)}, u32[]{:S(2)}, u32[]{:S(2)}) %all-to-all-start) | async-done | bytes 393248 | tf_op jit(solution)/shard_map/all_to_all | solution.py:289
  44.3 1.0 %copy-done.1 = bf16[2,192,640]{2,1,0:T(8,128)(2,1)S(1)} copy-done((bf16[2,192,640]{2,1,0:T(8,128)(2,1)S(1)}, bf16[2,192,640]{2,1,0:T(8,128)(2,1)}, u32[]{:S(2)}) %copy-start.1) | copy-done | bytes 491544
  45.4 7.3 %shard_map.31 = bf16[32,48,128]{2,1,0:T(8,128)(2,1)S(1)} custom-call(s32[3]{0:T(128)S(1)} %pad_add_fusion.place, bf16[32,48,128]{2,1,0:T(8,128)(2,1)S(1)} %all-to-all-done.q_ref, bf16[2,192,640]{2,1,0:T(8,128)(2,1)} %refs_0_.1, bf16[2,192,640]{2,1,0:T(8,128)(2,1)S(1)} %copy-done.1, bf16[2,192,640]{2,1,0:T(8,128)(2,1)S(1)} %collective-permute-done.1.refs_0_.refs_2_, ...), custom_call_target="tpu_custom_call" | custom-call | flops 1557135360 | bytes 5406720 | tf_op jit(solution)/shard_map/pallas_call | solution.py:230
  52.7 19.3 %all_to_all.15.x_ref = bf16[32,48,128]{2,1,0:T(8,128)(2,1)S(1)} all-to-all(bf16[32,48,128]{2,1,0:T(8,128)(2,1)S(1)} %shard_map.31), channel_id=1, replica_groups=mesh['zh'=4,'y'=4,'c'=2,'zl'=2,'x'=4] {'zh','x','zl'}, dimensions={0} | all-to-all | bytes 786432 | tf_op jit(solution)/shard_map/all_to_all | solution.py:289
  71.9 1.0 %shard_map.32 = bf16[9,5120]{1,0:T(8,128)(2,1)} custom-call(bf16[32,48,128]{2,1,0:T(8,128)(2,1)S(1)} %all_to_all.15.x_ref), custom_call_target="tpu_custom_call" | custom-call | tf_op jit(solution)/shard_map/pallas_call | solution.py:274
  (20 shorter events, 0.4 us)
Async XLA Ops:
  0.0 13.2 %collective-permute-start.1 = (bf16[2,192,640]{2,1,0:T(8,128)(2,1)}, bf16[2,192,640]{2,1,0:T(8,128)(2,1)S(1)}, u32[]{:S(2)}, u32[]{:S(2)}) collective-permute-start(bf16[2,192,640]{2,1,0:T(8,128)(2,1)} %refs_0_.1), channel_id=1, source_target_pairs={{0,16},{16,32},{32,48},{48,0},{1,17},{17,33},{33,49},{49,1},{2,18}... | collective-permute-start | bytes 1474568 | tf_op jit(solution)/shard_map/ppermute | solution.py:285
  1.6 13.3 %collective-permute-start.3 = (bf16[2,192,640]{2,1,0:T(8,128)(2,1)}, bf16[2,192,640]{2,1,0:T(8,128)(2,1)S(1)}, u32[]{:S(2)}, u32[]{:S(2)}) collective-permute-start(bf16[2,192,640]{2,1,0:T(8,128)(2,1)} %refs_0_.1), channel_id=1, source_target_pairs={{0,48},{16,0},{32,16},{48,32},{1,49},{17,1},{33,17},{49,33},{2,50}... | collective-permute-start | bytes 1474568 | tf_op jit(solution)/shard_map/ppermute | solution.py:285
  4.3 12.4 %all-to-all-start.1 = ((bf16[8,96,128]{2,1,0:T(8,128)(2,1)}), bf16[8,96,128]{2,1,0:T(8,128)(2,1)S(1)}, u32[]{:S(2)}, u32[]{:S(2)}) async-start(bf16[8,96,128]{2,1,0:T(8,128)(2,1)} %get-tuple-element.8), calls=%async_computation.1 | async-start | bytes 393216 | tf_op jit(solution)/shard_map/all_to_all | solution.py:289
  13.2 18.7 %collective-permute-start.5 = (bf16[192,640]{1,0:T(8,128)(2,1)S(1)}, bf16[192,640]{1,0:T(8,128)(2,1)S(1)}, u32[]{:S(2)}, u32[]{:S(2)}) collective-permute-start(bf16[192,640]{1,0:T(8,128)(2,1)S(1)} %slice_bitcast_fusion.1), channel_id=1, source_target_pairs={{0,16},{16,32},{32,48},{48,0},{1,17},{17,33},{33,49},{49,1},{2,18}... | collective-permute-start | bytes 737288 | tf_op jit(solution)/shard_map/ppermute | solution.py:285
  14.9 17.0 %collective-permute-start.7 = (bf16[192,640]{1,0:T(8,128)(2,1)S(1)}, bf16[192,640]{1,0:T(8,128)(2,1)S(1)}, u32[]{:S(2)}, u32[]{:S(2)}) collective-permute-start(bf16[192,640]{1,0:T(8,128)(2,1)S(1)} %slice_bitcast_fusion), channel_id=1, source_target_pairs={{0,48},{16,0},{32,16},{48,32},{1,49},{17,1},{33,17},{49,33},{2,50}... | collective-permute-start | bytes 737288 | tf_op jit(solution)/shard_map/ppermute | solution.py:285
  16.7 15.0 %collective-permute-start.11 = (bf16[8,96,128]{2,1,0:T(8,128)(2,1)S(1)}, bf16[8,96,128]{2,1,0:T(8,128)(2,1)S(1)}, u32[]{:S(2)}, u32[]{:S(2)}) collective-permute-start(bf16[8,96,128]{2,1,0:T(8,128)(2,1)S(1)} %shard_map.29.refs_0_), channel_id=1, source_target_pairs={{0,48},{16,0},{32,16},{48,32},{1,49},{17,1},{33,17},{49,33},{2,50}... | collective-permute-start | bytes 589832 | tf_op jit(solution)/shard_map/ppermute | solution.py:285
  18.5 13.4 %collective-permute-start.10 = (bf16[8,96,128]{2,1,0:T(8,128)(2,1)S(1)}, bf16[8,96,128]{2,1,0:T(8,128)(2,1)S(1)}, u32[]{:S(2)}, u32[]{:S(2)}) collective-permute-start(bf16[8,96,128]{2,1,0:T(8,128)(2,1)S(1)} %shard_map.29.refs_0_), channel_id=1, source_target_pairs={{0,32},{16,48},{32,0},{48,16},{1,33},{17,49},{33,1},{49,17},{2,34}... | collective-permute-start | bytes 589832 | tf_op jit(solution)/shard_map/ppermute | solution.py:285
  19.8 12.0 %collective-permute-start.9 = (bf16[8,96,128]{2,1,0:T(8,128)(2,1)S(1)}, bf16[8,96,128]{2,1,0:T(8,128)(2,1)S(1)}, u32[]{:S(2)}, u32[]{:S(2)}) collective-permute-start(bf16[8,96,128]{2,1,0:T(8,128)(2,1)S(1)} %shard_map.29.refs_0_), channel_id=1, source_target_pairs={{0,16},{16,32},{32,48},{48,0},{1,17},{17,33},{33,49},{49,1},{2,18}... | collective-permute-start | bytes 589832 | tf_op jit(solution)/shard_map/ppermute | solution.py:285
  21.7 22.6 %all-to-all-start = ((bf16[32,48,128]{2,1,0:T(8,128)(2,1)}), bf16[32,48,128]{2,1,0:T(8,128)(2,1)S(1)}, u32[]{:S(2)}, u32[]{:S(2)}) async-start(bf16[32,48,128]{2,1,0:T(8,128)(2,1)} %get-tuple-element.7), calls=%async_computation | async-start | bytes 786432 | tf_op jit(solution)/shard_map/all_to_all | solution.py:289
  31.8 3.3 %collective-permute-start = (bf16[2,192,640]{2,1,0:T(8,128)(2,1)}, bf16[2,192,640]{2,1,0:T(8,128)(2,1)S(1)}, u32[]{:S(2)}, u32[]{:S(2)}) collective-permute-start(bf16[2,192,640]{2,1,0:T(8,128)(2,1)} %refs_0_.1), channel_id=1, source_target_pairs={{0,8},{8,0},{1,9},{9,1},{2,10},{10,2},{3,11},{11,3},{4,12},{12,4},... | collective-permute-start | bytes 1474568 | tf_op jit(solution)/shard_map/ppermute | solution.py:285
  33.9 10.4 %collective-permute-start.12 = (bf16[2,288,640]{2,1,0:T(8,128)(2,1)S(1)}, bf16[2,288,640]{2,1,0:T(8,128)(2,1)S(1)}, u32[]{:S(2)}, u32[]{:S(2)}) collective-permute-start(bf16[2,288,640]{2,1,0:T(8,128)(2,1)S(1)} %shard_map.30.refs_10_), channel_id=1, source_target_pairs={{0,8},{8,0},{1,9},{9,1},{2,10},{10,2},{3,11},{11,3},{4,12},{12,4},... | collective-permute-start | bytes 2211848 | tf_op jit(solution)/shard_map/ppermute | solution.py:285
  34.5 9.8 %collective-permute-start.2 = (bf16[2,192,640]{2,1,0:T(8,128)(2,1)S(1)}, bf16[2,192,640]{2,1,0:T(8,128)(2,1)}, u32[]{:S(2)}, u32[]{:S(2)}) collective-permute-start(bf16[2,192,640]{2,1,0:T(8,128)(2,1)S(1)} %collective-permute-done.1.refs_0_.refs_2_), channel_id=1, source_target_pairs={{0,8},{8,0},{1,9},{9,1},{2,10},{10,2},{3,11},{11,3},{4,12},{12,4},... | collective-permute-start | bytes 1474568 | tf_op jit(solution)/shard_map/ppermute | solution.py:285
  34.6 9.7 %collective-permute-start.4 = (bf16[2,192,640]{2,1,0:T(8,128)(2,1)S(1)}, bf16[2,192,640]{2,1,0:T(8,128)(2,1)}, u32[]{:S(2)}, u32[]{:S(2)}) collective-permute-start(bf16[2,192,640]{2,1,0:T(8,128)(2,1)S(1)} %collective-permute-done.3.refs_1_.refs_4_), channel_id=1, source_target_pairs={{0,8},{8,0},{1,9},{9,1},{2,10},{10,2},{3,11},{11,3},{4,12},{12,4},... | collective-permute-start | bytes 1474568 | tf_op jit(solution)/shard_map/ppermute | solution.py:285
  35.0 9.3 %collective-permute-start.6 = (bf16[192,640]{1,0:T(8,128)(2,1)S(1)}, bf16[192,640]{1,0:T(8,128)(2,1)}, u32[]{:S(2)}, u32[]{:S(2)}) collective-permute-start(bf16[192,640]{1,0:T(8,128)(2,1)S(1)} %collective-permute-done.5.refs_4_.refs_6_), channel_id=1, source_target_pairs={{0,8},{8,0},{1,9},{9,1},{2,10},{10,2},{3,11},{11,3},{4,12},{12,4},... | collective-permute-start | bytes 737288 | tf_op jit(solution)/shard_map/ppermute | solution.py:285
  35.1 0.8 %copy-start = (bf16[2,192,640]{2,1,0:T(8,128)(2,1)}, bf16[2,192,640]{2,1,0:T(8,128)(2,1)S(1)}, u32[]{:S(2)}) copy-start(bf16[2,192,640]{2,1,0:T(8,128)(2,1)S(1)} %collective-permute-done.refs_1_) | copy-start | bytes 1474564
  35.9 8.4 %collective-permute-start.8 = (bf16[192,640]{1,0:T(8,128)(2,1)S(1)}, bf16[192,640]{1,0:T(8,128)(2,1)}, u32[]{:S(2)}, u32[]{:S(2)}) collective-permute-start(bf16[192,640]{1,0:T(8,128)(2,1)S(1)} %collective-permute-done.7.refs_5_.refs_8_), channel_id=1, source_target_pairs={{0,8},{8,0},{1,9},{9,1},{2,10},{10,2},{3,11},{11,3},{4,12},{12,4},... | collective-permute-start | bytes 737288 | tf_op jit(solution)/shard_map/ppermute | solution.py:285
  44.3 1.0 %copy-start.1 = (bf16[2,192,640]{2,1,0:T(8,128)(2,1)S(1)}, bf16[2,192,640]{2,1,0:T(8,128)(2,1)}, u32[]{:S(2)}) copy-start(bf16[2,192,640]{2,1,0:T(8,128)(2,1)} %copy-done) | copy-start | bytes 1474564

commit v5 on v4

--- a/solution.py
+++ b/solution.py
@@ -32,7 +32,7 @@
 SKEYS = NY * NG * HOME
 KEYS = NHIST + NC * SKEYS
 PIECES = 10
-HEAD_PARTS = ((0, 2), (2, 5))
+HEAD_PARTS = ((0, 1), (1, 5))
 SCALE = math.log2(math.e) / math.sqrt(HEAD_DIM)
 F32, BF16 = jnp.float32, jnp.bfloat16
 

time: 73.9 us -> 73.3 us (level)
  no operation moved by 1% of the time
where the time goes in v5:
time: 73.3 us; the launch traced here: 72.4 us
  starting transfers between devices  26.6 us (36%)
  blocking collectives  19.3 us (26%)
  waiting for transfers between devices  12.6 us (17%)
  Pallas kernels  10.7 us (15%)
  local copies, waits for them, and re-layouts  2.99 us (4%)
    all_to_all x1, blocking collectives, exchange(): return lax.all_to_all(x, axes, split_axis=0, concat_axis=0, tiled=True)  19.3 us
    all_to_all x2, starting transfers between devices, exchange(): return lax.all_to_all(x, axes, split_axis=0, concat_axis=0, tiled=True)  15.5 us
    ppermute x13, starting transfers between devices, from_back(): return lax.ppermute(x, axis, [(i, (i + back) % size) for i in range(size)])  11 us
    all_to_all x2, waiting for transfers between devices, exchange(): return lax.all_to_all(x, axes, split_axis=0, concat_axis=0, tiled=True)  9.19 us
    pallas_call x1, Pallas kernels, attend(): pl.pallas_call(attend_kernel, out_shape=jax.ShapeDtypeStruct((CHUNKS, CHU...  6.74 us
    ppermute x13, waiting for transfers between devices, from_back(): return lax.ppermute(x, axis, [(i, (i + back) % size) for i in range(size)])  3.43 us
    unnamed x5, local copies, waits for them, and re-layouts  2.95 us
    pallas_call x1, Pallas kernels, sort_span(): pl.pallas_call(sort_kernel, out_shape=jax.ShapeDtypeStruct((2, SKEYS, WID...  2.01 us
  transfers between devices with their start and end apart: 15, of which 3 were waited for; matrix products, arithmetic and copies ran while one was open for 2% of the time, Pallas kernels for 4%

profile of v5, /device:TPU:8, one launch (start us, length us, event | category | flops | bytes accessed | tf_op | source)
XLA Modules:
  0.0 72.4 jit_solution(5611076561953739596)
XLA Ops:
  0.0 1.6 %collective-permute-start.1 = (bf16[2,192,640]{2,1,0:T(8,128)(2,1)}, bf16[2,192,640]{2,1,0:T(8,128)(2,1)S(1)}, u32[]{:S(2)}, u32[]{:S(2)}) collective-permute-start(bf16[2,192,640]{2,1,0:T(8,128)(2,1)} %refs_0_.1), channel_id=1, source_target_pairs={{0,16},{16,32},{32,48},{48,0},{1,17},{17,33},{33,49},{49,1},{2,18}... | collective-permute-start | bytes 1474568 | tf_op jit(solution)/shard_map/ppermute | solution.py:285
  1.6 0.6 collective-permute-start.3
  2.2 1.1 %copy.3.x_ref = bf16[3,9,5120]{2,1,0:T(8,128)(2,1)S(1)} copy(bf16[3,9,5120]{2,0,1:T(4,128)(2,1)} %param.2) | data formatting | bytes 552960 | tf_op args[0]
  3.3 1.0 %shard_map.28 = (bf16[32,48,128]{2,1,0:T(8,128)(2,1)}, bf16[8,96,128]{2,1,0:T(8,128)(2,1)}) custom-call(bf16[3,9,5120]{2,1,0:T(8,128)(2,1)S(1)} %copy.3.x_ref), custom_call_target="tpu_custom_call" | custom-call | tf_op jit(solution)/shard_map/pallas_call | solution.py:73
  4.3 5.5 %all-to-all-start.1 = ((bf16[8,96,128]{2,1,0:T(8,128)(2,1)}), bf16[8,96,128]{2,1,0:T(8,128)(2,1)S(1)}, u32[]{:S(2)}, u32[]{:S(2)}) async-start(bf16[8,96,128]{2,1,0:T(8,128)(2,1)} %get-tuple-element.8), calls=%async_computation.1 | async-start | bytes 393216 | tf_op jit(solution)/shard_map/all_to_all | solution.py:289
  9.8 3.4 %collective-permute-done.1.refs_0_.refs_2_ = bf16[2,192,640]{2,1,0:T(8,128)(2,1)S(1)} collective-permute-done((bf16[2,192,640]{2,1,0:T(8,128)(2,1)}, bf16[2,192,640]{2,1,0:T(8,128)(2,1)S(1)}, u32[]{:S(2)}, u32[]{:S(2)}) %collective-permute-start.1) | collective-permute-done | bytes 491552 | tf_op jit(solution)/shard_map/ppermute | solution.py:285
  13.2 1.7 %collective-permute-start.5 = (bf16[192,640]{1,0:T(8,128)(2,1)S(1)}, bf16[192,640]{1,0:T(8,128)(2,1)S(1)}, u32[]{:S(2)}, u32[]{:S(2)}) collective-permute-start(bf16[192,640]{1,0:T(8,128)(2,1)S(1)} %slice_bitcast_fusion.1), channel_id=1, source_target_pairs={{0,16},{16,32},{32,48},{48,0},{1,17},{17,33},{33,49},{49,1},{2,18}... | collective-permute-start | bytes 737288 | tf_op jit(solution)/shard_map/ppermute | solution.py:285
  14.9 0.5 collective-permute-start.7
  15.4 1.3 %all-to-all-done.1.x_ref = bf16[8,96,128]{2,1,0:T(8,128)(2,1)S(1)} async-done(((bf16[8,96,128]{2,1,0:T(8,128)(2,1)}), bf16[8,96,128]{2,1,0:T(8,128)(2,1)S(1)}, u32[]{:S(2)}, u32[]{:S(2)}) %all-to-all-start.1) | async-done | bytes 196640 | tf_op jit(solution)/shard_map/all_to_all | solution.py:289
  16.7 1.7 %collective-permute-start.11 = (bf16[8,96,128]{2,1,0:T(8,128)(2,1)S(1)}, bf16[8,96,128]{2,1,0:T(8,128)(2,1)S(1)}, u32[]{:S(2)}, u32[]{:S(2)}) collective-permute-start(bf16[8,96,128]{2,1,0:T(8,128)(2,1)S(1)} %shard_map.29.refs_0_), channel_id=1, source_target_pairs={{0,48},{16,0},{32,16},{48,32},{1,49},{17,1},{33,17},{49,33},{2,50}... | collective-permute-start | bytes 589832 | tf_op jit(solution)/shard_map/ppermute | solution.py:285
  18.5 1.4 %collective-permute-start.10 = (bf16[8,96,128]{2,1,0:T(8,128)(2,1)S(1)}, bf16[8,96,128]{2,1,0:T(8,128)(2,1)S(1)}, u32[]{:S(2)}, u32[]{:S(2)}) collective-permute-start(bf16[8,96,128]{2,1,0:T(8,128)(2,1)S(1)} %shard_map.29.refs_0_), channel_id=1, source_target_pairs={{0,32},{16,48},{32,0},{48,16},{1,33},{17,49},{33,1},{49,17},{2,34}... | collective-permute-start | bytes 589832 | tf_op jit(solution)/shard_map/ppermute | solution.py:285
  19.8 1.9 %collective-permute-start.9 = (bf16[8,96,128]{2,1,0:T(8,128)(2,1)S(1)}, bf16[8,96,128]{2,1,0:T(8,128)(2,1)S(1)}, u32[]{:S(2)}, u32[]{:S(2)}) collective-permute-start(bf16[8,96,128]{2,1,0:T(8,128)(2,1)S(1)} %shard_map.29.refs_0_), channel_id=1, source_target_pairs={{0,16},{16,32},{32,48},{48,0},{1,17},{17,33},{33,49},{49,1},{2,18}... | collective-permute-start | bytes 589832 | tf_op jit(solution)/shard_map/ppermute | solution.py:285
  21.7 10.0 %all-to-all-start = ((bf16[32,48,128]{2,1,0:T(8,128)(2,1)}), bf16[32,48,128]{2,1,0:T(8,128)(2,1)S(1)}, u32[]{:S(2)}, u32[]{:S(2)}) async-start(bf16[32,48,128]{2,1,0:T(8,128)(2,1)} %get-tuple-element.7), calls=%async_computation | async-start | bytes 786432 | tf_op jit(solution)/shard_map/all_to_all | solution.py:289
  31.9 2.0 %shard_map.30.refs_10_ = bf16[2,288,640]{2,1,0:T(8,128)(2,1)S(1)} custom-call(bf16[8,96,128]{2,1,0:T(8,128)(2,1)S(1)} %shard_map.29.refs_0_, bf16[8,96,128]{2,1,0:T(8,128)(2,1)S(1)} %collective-permute-done.9.refs_1_, bf16[8,96,128]{2,1,0:T(8,128)(2,1)S(1)} %collective-permute-done.10.refs_2_, bf16[8,96,128]{2,1,0:T(8,128)(2,1)S(1)} %collective-permute-done.11.refs_3_, ...), custom_call_target="tpu_custom_call" | custom-call | tf_op jit(solution)/shard_map/pallas_call | solution.py:126
  33.9 0.6 collective-permute-start.12
  34.5 0.1 collective-permute-start.2
  34.6 0.4 collective-permute-start.4
  35.1 0.8 %copy-done = bf16[2,192,640]{2,1,0:T(8,128)(2,1)} copy-done((bf16[2,192,640]{2,1,0:T(8,128)(2,1)}, bf16[2,192,640]{2,1,0:T(8,128)(2,1)S(1)}, u32[]{:S(2)}) %copy-start) | copy-done | bytes 491544
  35.9 0.4 collective-permute-start.8
  36.4 7.9 %all-to-all-done.q_ref = bf16[32,48,128]{2,1,0:T(8,128)(2,1)S(1)} async-done(((bf16[32,48,128]{2,1,0:T(8,128)(2,1)}), bf16[32,48,128]{2,1,0:T(8,128)(2,1)S(1)}, u32[]{:S(2)}, u32[]{:S(2)}) %all-to-all-start) | async-done | bytes 393248 | tf_op jit(solution)/shard_map/all_to_all | solution.py:289
  44.3 1.0 %copy-done.1 = bf16[2,192,640]{2,1,0:T(8,128)(2,1)S(1)} copy-done((bf16[2,192,640]{2,1,0:T(8,128)(2,1)S(1)}, bf16[2,192,640]{2,1,0:T(8,128)(2,1)}, u32[]{:S(2)}) %copy-start.1) | copy-done | bytes 491544
  45.4 6.7 %shard_map.31 = bf16[32,48,128]{2,1,0:T(8,128)(2,1)S(1)} custom-call(s32[3]{0:T(128)S(1)} %pad_add_fusion.place, bf16[32,48,128]{2,1,0:T(8,128)(2,1)S(1)} %all-to-all-done.q_ref, bf16[2,192,640]{2,1,0:T(8,128)(2,1)} %refs_0_.1, bf16[2,192,640]{2,1,0:T(8,128)(2,1)S(1)} %copy-done.1, bf16[2,192,640]{2,1,0:T(8,128)(2,1)S(1)} %collective-permute-done.1.refs_0_.refs_2_, ...), custom_call_target="tpu_custom_call" | custom-call | flops 1557135360 | bytes 5406720 | tf_op jit(solution)/shard_map/pallas_call | solution.py:230
  52.1 19.3 %all_to_all.15.x_ref = bf16[32,48,128]{2,1,0:T(8,128)(2,1)S(1)} all-to-all(bf16[32,48,128]{2,1,0:T(8,128)(2,1)S(1)} %shard_map.31), channel_id=1, replica_groups=mesh['zh'=4,'y'=4,'c'=2,'zl'=2,'x'=4] {'zh','x','zl'}, dimensions={0} | all-to-all | bytes 786432 | tf_op jit(solution)/shard_map/all_to_all | solution.py:289
  71.4 1.0 %shard_map.32 = bf16[9,5120]{1,0:T(8,128)(2,1)} custom-call(bf16[32,48,128]{2,1,0:T(8,128)(2,1)S(1)} %all_to_all.15.x_ref), custom_call_target="tpu_custom_call" | custom-call | tf_op jit(solution)/shard_map/pallas_call | solution.py:274
  (20 shorter events, 0.4 us)
Async XLA Ops:
  0.0 13.2 %collective-permute-start.1 = (bf16[2,192,640]{2,1,0:T(8,128)(2,1)}, bf16[2,192,640]{2,1,0:T(8,128)(2,1)S(1)}, u32[]{:S(2)}, u32[]{:S(2)}) collective-permute-start(bf16[2,192,640]{2,1,0:T(8,128)(2,1)} %refs_0_.1), channel_id=1, source_target_pairs={{0,16},{16,32},{32,48},{48,0},{1,17},{17,33},{33,49},{49,1},{2,18}... | collective-permute-start | bytes 1474568 | tf_op jit(solution)/shard_map/ppermute | solution.py:285
  1.6 13.3 %collective-permute-start.3 = (bf16[2,192,640]{2,1,0:T(8,128)(2,1)}, bf16[2,192,640]{2,1,0:T(8,128)(2,1)S(1)}, u32[]{:S(2)}, u32[]{:S(2)}) collective-permute-start(bf16[2,192,640]{2,1,0:T(8,128)(2,1)} %refs_0_.1), channel_id=1, source_target_pairs={{0,48},{16,0},{32,16},{48,32},{1,49},{17,1},{33,17},{49,33},{2,50}... | collective-permute-start | bytes 1474568 | tf_op jit(solution)/shard_map/ppermute | solution.py:285
  4.3 12.4 %all-to-all-start.1 = ((bf16[8,96,128]{2,1,0:T(8,128)(2,1)}), bf16[8,96,128]{2,1,0:T(8,128)(2,1)S(1)}, u32[]{:S(2)}, u32[]{:S(2)}) async-start(bf16[8,96,128]{2,1,0:T(8,128)(2,1)} %get-tuple-element.8), calls=%async_computation.1 | async-start | bytes 393216 | tf_op jit(solution)/shard_map/all_to_all | solution.py:289
  13.2 18.7 %collective-permute-start.5 = (bf16[192,640]{1,0:T(8,128)(2,1)S(1)}, bf16[192,640]{1,0:T(8,128)(2,1)S(1)}, u32[]{:S(2)}, u32[]{:S(2)}) collective-permute-start(bf16[192,640]{1,0:T(8,128)(2,1)S(1)} %slice_bitcast_fusion.1), channel_id=1, source_target_pairs={{0,16},{16,32},{32,48},{48,0},{1,17},{17,33},{33,49},{49,1},{2,18}... | collective-permute-start | bytes 737288 | tf_op jit(solution)/shard_map/ppermute | solution.py:285
  14.9 17.0 %collective-permute-start.7 = (bf16[192,640]{1,0:T(8,128)(2,1)S(1)}, bf16[192,640]{1,0:T(8,128)(2,1)S(1)}, u32[]{:S(2)}, u32[]{:S(2)}) collective-permute-start(bf16[192,640]{1,0:T(8,128)(2,1)S(1)} %slice_bitcast_fusion), channel_id=1, source_target_pairs={{0,48},{16,0},{32,16},{48,32},{1,49},{17,1},{33,17},{49,33},{2,50}... | collective-permute-start | bytes 737288 | tf_op jit(solution)/shard_map/ppermute | solution.py:285
  16.7 15.0 %collective-permute-start.11 = (bf16[8,96,128]{2,1,0:T(8,128)(2,1)S(1)}, bf16[8,96,128]{2,1,0:T(8,128)(2,1)S(1)}, u32[]{:S(2)}, u32[]{:S(2)}) collective-permute-start(bf16[8,96,128]{2,1,0:T(8,128)(2,1)S(1)} %shard_map.29.refs_0_), channel_id=1, source_target_pairs={{0,48},{16,0},{32,16},{48,32},{1,49},{17,1},{33,17},{49,33},{2,50}... | collective-permute-start | bytes 589832 | tf_op jit(solution)/shard_map/ppermute | solution.py:285
  18.5 13.4 %collective-permute-start.10 = (bf16[8,96,128]{2,1,0:T(8,128)(2,1)S(1)}, bf16[8,96,128]{2,1,0:T(8,128)(2,1)S(1)}, u32[]{:S(2)}, u32[]{:S(2)}) collective-permute-start(bf16[8,96,128]{2,1,0:T(8,128)(2,1)S(1)} %shard_map.29.refs_0_), channel_id=1, source_target_pairs={{0,32},{16,48},{32,0},{48,16},{1,33},{17,49},{33,1},{49,17},{2,34}... | collective-permute-start | bytes 589832 | tf_op jit(solution)/shard_map/ppermute | solution.py:285
  19.8 12.0 %collective-permute-start.9 = (bf16[8,96,128]{2,1,0:T(8,128)(2,1)S(1)}, bf16[8,96,128]{2,1,0:T(8,128)(2,1)S(1)}, u32[]{:S(2)}, u32[]{:S(2)}) collective-permute-start(bf16[8,96,128]{2,1,0:T(8,128)(2,1)S(1)} %shard_map.29.refs_0_), channel_id=1, source_target_pairs={{0,16},{16,32},{32,48},{48,0},{1,17},{17,33},{33,49},{49,1},{2,18}... | collective-permute-start | bytes 589832 | tf_op jit(solution)/shard_map/ppermute | solution.py:285
  21.7 22.6 %all-to-all-start = ((bf16[32,48,128]{2,1,0:T(8,128)(2,1)}), bf16[32,48,128]{2,1,0:T(8,128)(2,1)S(1)}, u32[]{:S(2)}, u32[]{:S(2)}) async-start(bf16[32,48,128]{2,1,0:T(8,128)(2,1)} %get-tuple-element.7), calls=%async_computation | async-start | bytes 786432 | tf_op jit(solution)/shard_map/all_to_all | solution.py:289
  31.8 3.3 %collective-permute-start = (bf16[2,192,640]{2,1,0:T(8,128)(2,1)}, bf16[2,192,640]{2,1,0:T(8,128)(2,1)S(1)}, u32[]{:S(2)}, u32[]{:S(2)}) collective-permute-start(bf16[2,192,640]{2,1,0:T(8,128)(2,1)} %refs_0_.1), channel_id=1, source_target_pairs={{0,8},{8,0},{1,9},{9,1},{2,10},{10,2},{3,11},{11,3},{4,12},{12,4},... | collective-permute-start | bytes 1474568 | tf_op jit(solution)/shard_map/ppermute | solution.py:285
  33.9 10.4 %collective-permute-start.12 = (bf16[2,288,640]{2,1,0:T(8,128)(2,1)S(1)}, bf16[2,288,640]{2,1,0:T(8,128)(2,1)S(1)}, u32[]{:S(2)}, u32[]{:S(2)}) collective-permute-start(bf16[2,288,640]{2,1,0:T(8,128)(2,1)S(1)} %shard_map.30.refs_10_), channel_id=1, source_target_pairs={{0,8},{8,0},{1,9},{9,1},{2,10},{10,2},{3,11},{11,3},{4,12},{12,4},... | collective-permute-start | bytes 2211848 | tf_op jit(solution)/shard_map/ppermute | solution.py:285
  34.5 9.8 %collective-permute-start.2 = (bf16[2,192,640]{2,1,0:T(8,128)(2,1)S(1)}, bf16[2,192,640]{2,1,0:T(8,128)(2,1)}, u32[]{:S(2)}, u32[]{:S(2)}) collective-permute-start(bf16[2,192,640]{2,1,0:T(8,128)(2,1)S(1)} %collective-permute-done.1.refs_0_.refs_2_), channel_id=1, source_target_pairs={{0,8},{8,0},{1,9},{9,1},{2,10},{10,2},{3,11},{11,3},{4,12},{12,4},... | collective-permute-start | bytes 1474568 | tf_op jit(solution)/shard_map/ppermute | solution.py:285
  34.6 9.7 %collective-permute-start.4 = (bf16[2,192,640]{2,1,0:T(8,128)(2,1)S(1)}, bf16[2,192,640]{2,1,0:T(8,128)(2,1)}, u32[]{:S(2)}, u32[]{:S(2)}) collective-permute-start(bf16[2,192,640]{2,1,0:T(8,128)(2,1)S(1)} %collective-permute-done.3.refs_1_.refs_4_), channel_id=1, source_target_pairs={{0,8},{8,0},{1,9},{9,1},{2,10},{10,2},{3,11},{11,3},{4,12},{12,4},... | collective-permute-start | bytes 1474568 | tf_op jit(solution)/shard_map/ppermute | solution.py:285
  35.0 9.3 %collective-permute-start.6 = (bf16[192,640]{1,0:T(8,128)(2,1)S(1)}, bf16[192,640]{1,0:T(8,128)(2,1)}, u32[]{:S(2)}, u32[]{:S(2)}) collective-permute-start(bf16[192,640]{1,0:T(8,128)(2,1)S(1)} %collective-permute-done.5.refs_4_.refs_6_), channel_id=1, source_target_pairs={{0,8},{8,0},{1,9},{9,1},{2,10},{10,2},{3,11},{11,3},{4,12},{12,4},... | collective-permute-start | bytes 737288 | tf_op jit(solution)/shard_map/ppermute | solution.py:285
  35.1 0.8 %copy-start = (bf16[2,192,640]{2,1,0:T(8,128)(2,1)}, bf16[2,192,640]{2,1,0:T(8,128)(2,1)S(1)}, u32[]{:S(2)}) copy-start(bf16[2,192,640]{2,1,0:T(8,128)(2,1)S(1)} %collective-permute-done.refs_1_) | copy-start | bytes 1474564
  35.9 8.4 %collective-permute-start.8 = (bf16[192,640]{1,0:T(8,128)(2,1)S(1)}, bf16[192,640]{1,0:T(8,128)(2,1)}, u32[]{:S(2)}, u32[]{:S(2)}) collective-permute-start(bf16[192,640]{1,0:T(8,128)(2,1)S(1)} %collective-permute-done.7.refs_5_.refs_8_), channel_id=1, source_target_pairs={{0,8},{8,0},{1,9},{9,1},{2,10},{10,2},{3,11},{11,3},{4,12},{12,4},... | collective-permute-start | bytes 737288 | tf_op jit(solution)/shard_map/ppermute | solution.py:285
  44.3 1.0 %copy-start.1 = (bf16[2,192,640]{2,1,0:T(8,128)(2,1)S(1)}, bf16[2,192,640]{2,1,0:T(8,128)(2,1)}, u32[]{:S(2)}) copy-start(bf16[2,192,640]{2,1,0:T(8,128)(2,1)} %copy-done) | copy-start | bytes 1474564
